TPU v7x, 32 devices: a whole 2x2x4 slice. The times are simulated.
32 devices in a mesh: row: 4 (over z), inst: 8 (over y, x, core).
Axes of the slice: x: 2, y: 2, z: 4, core: 2. Of those that a mesh axis runs over, the one named last changes fastest.
Arguments:
- design: bfloat16 [8192, 16384], P('row', 'inst'), may hold values from -0.046875 to 0.046875
- labels: int32 [8192, 256], P('row'), may hold values 0 or 1
- saved_logits: float32 [3, 8192, 256], P(None, 'row'), may hold values from -8 to 8
- saved_coefficients: bfloat16 [3, 16384, 256], P(None, 'inst'), may hold values from -6 to 6
- cotangent: float32 [16384, 256], P('inst'), may hold values from -2 to 2
Outputs:
- first_adjoint: float32 [16384, 256], P('inst')
- design_grad: float32 [8192, 16384], P('row', 'inst')
All inputs are finite; a program needn't handle non-finite values. No bound on the sum of `labels` on one device may be relied on, other than what follows from the above.
Results may differ from a plain program's by a relative error of at most 0.0026.
Values may be sent and summed in bfloat16 or wider, within the bound.
No kernel may reach another device: no remote copies, remote signals or barrier semaphores. Data moves between devices by JAX's collectives and lax.ppermute only.
A program may use at most 192 MiB of HBM per device.

v0:
```python
import jax
import jax.numpy as jnp
from jax import lax
from jax.sharding import PartitionSpec as P


def shards(design, labels, saved_logits, saved_coefficients, cotangent):
    step_rate = 2.0
    adjoint = cotangent
    accum = jnp.zeros(design.shape, jnp.float32)
    targets = labels.astype(jnp.float32)
    count_steps = saved_logits.shape[0]
    for step in range(count_steps - 1, -1, -1):
        adjoint_low = adjoint.astype(jnp.bfloat16)
        local_sum = jnp.dot(design, adjoint_low, preferred_element_type=jnp.float32)
        probability = jax.nn.sigmoid(saved_logits[step])
        curvature = probability * (1.0 - probability)
        residual = (probability - targets).astype(jnp.bfloat16)
        accum = accum + jnp.dot(residual, adjoint_low.T, preferred_element_type=jnp.float32)
        product = lax.psum(local_sum, "inst")
        weighted = (curvature * product).astype(jnp.bfloat16)
        accum = accum + jnp.dot(
            weighted, saved_coefficients[step].T, preferred_element_type=jnp.float32
        )
        local_hess = lax.dot_general(
            design, weighted, (((0,), (0,)), ((), ())), preferred_element_type=jnp.float32
        )
        hessian_term = lax.psum(local_hess, "row")
        adjoint = adjoint - step_rate * hessian_term
    return (adjoint, -step_rate * accum)


def solution(mesh):
    placed = (
        P("row", "inst"),
        P("row", None),
        P(None, "row", None),
        P(None, "inst", None),
        P("inst", None),
    )
    return jax.shard_map(
        shards,
        mesh=mesh,
        in_specs=placed,
        out_specs=(P("inst", None), P("row", "inst")),
        check_vma=False,
    )
```

profile of v0, /device:TPU:0, one launch (start us, length us, event | category | flops | bytes accessed | tf_op | source)
XLA Modules:
  0.0 523.8 jit_solution(4867219622418435826)
XLA Ops:
  7.2 0.0 all-reduce.7.cloned.1.call-start
  7.2 7.7 %fusion.27 = f32[2048,256]{1,0:T(8,128)} fusion(bf16[2048,2048]{1,0:T(8,128)(2,1)} %param.5, f32[2048,256]{1,0:T(8,128)} %param.9), kind=kOutput, calls=%fused_computation.42 | convolution fusion | flops 2148007936 | bytes 12582912 | tf_op jit(solution)/shard_map/dot_general | solution.py:15
  14.9 0.0 all-reduce.7.cloned.1.call-update
  14.9 0.0 all-reduce.9.cloned.1.call-start
  14.9 64.2 %all-reduce.7.cloned.1.call-done = f32[2048,256]{1,0:T(8,128)} async-done(((f32[2048,256]{1,0:T(8,128)}), f32[2048,256]{1,0:T(8,128)}) %all-reduce.7.cloned.1.call-update) | async-done | bytes 2097168 | tf_op jit(solution)/shard_map/psum | solution.py:20
  79.1 2.9 fusion.1
  82.0 7.0 %convolution_bitcast_fusion.4 = f32[2048,256]{0,1:T(8,128)} fusion(bf16[2048,256]{1,0:T(8,128)(2,1)S(1)} %fusion.1, bf16[2048,2048]{1,0:T(8,128)(2,1)} %param.5), kind=kOutput, calls=%fused_computation.8 | convolution fusion | flops 2147483648 | bytes 11534336 | tf_op jit(solution)/shard_map/dot_general | solution.py:25
  89.0 0.0 all-reduce.9.cloned.1.call-update
  89.1 0.0 all-reduce.11.cloned.1.call-start
  89.1 1.9 copy.7
  91.1 0.0 copy-start.4
  91.1 83.9 %all-reduce.9.cloned.1.call-done = f32[2048,256]{0,1:T(8,128)} async-done(((f32[2048,256]{0,1:T(8,128)}), f32[2048,256]{0,1:T(8,128)}) %all-reduce.9.cloned.1.call-update) | async-done | bytes 2097168 | tf_op jit(solution)/shard_map/psum | solution.py:28
  174.9 1.9 fusion.23
  176.9 0.0 copy-done.4
  176.9 1.0 copy-done.7
  177.9 7.1 %convolution_bitcast_fusion.3 = f32[2048,256]{1,0:T(8,128)} fusion(bf16[2048,256]{0,1:T(8,128)(2,1)S(1)} %fusion.23, bf16[2048,2048]{1,0:T(8,128)(2,1)} %param.5), kind=kOutput, calls=%fused_computation.7 | convolution fusion | flops 2147483648 | bytes 11534336 | tf_op jit(solution)/shard_map/dot_general | solution.py:15
  185.0 0.0 all-reduce.11.cloned.1.call-update
  185.0 0.0 all-reduce.13.cloned.1.call-start
  185.1 60.5 %all-reduce.11.cloned.1.call-done = f32[2048,256]{1,0:T(8,128)} async-done(((f32[2048,256]{1,0:T(8,128)}), f32[2048,256]{1,0:T(8,128)}) %all-reduce.11.cloned.1.call-update) | async-done | bytes 2097168 | tf_op jit(solution)/shard_map/psum | solution.py:20
  245.5 2.9 fusion.3
  248.4 0.0 copy-start.5
  248.4 1.0 copy-done.5
  249.4 7.1 %convolution_bitcast_fusion.2 = f32[2048,256]{0,1:T(8,128)} fusion(bf16[2048,256]{1,0:T(8,128)(2,1)S(1)} %fusion.3, bf16[2048,2048]{1,0:T(8,128)(2,1)} %param.5), kind=kOutput, calls=%fused_computation.6 | convolution fusion | flops 2147483648 | bytes 11534336 | tf_op jit(solution)/shard_map/dot_general | solution.py:25
  256.4 0.0 all-reduce.13.cloned.1.call-update
  256.5 0.2 all-reduce.15.cloned.1.call-start
  256.7 1.3 copy-done
  258.0 10.3 %fusion.9 = f32[2048,2048]{1,0:T(8,128)} fusion(s32[2048,256]{1,0:T(8,128)S(1)} %copy-done, f32[2048,256]{1,0:T(8,128)} %param.9, f32[3,2048,256]{2,1,0:T(8,128)} %param.7), kind=kOutput, calls=%fused_computation.27 | convolution fusion | flops 2151153664 | bytes 23068672 | tf_op jit(solution)/shard_map/dot_general | solution.py:19
  268.4 9.4 %fusion.18 = f32[2048,2048]{1,0:T(8,128)} fusion(bf16[2048,256]{1,0:T(8,128)(2,1)S(1)} %fusion.1, bf16[3,2048,256]{2,1,0:T(8,128)(2,1)} %param.8), kind=kOutput, calls=%fused_computation.33 | convolution fusion | flops 2147483648 | bytes 18874368 | tf_op jit(solution)/shard_map/dot_general | solution.py:22
  277.8 9.7 %fusion.11 = f32[2048,2048]{1,0:T(8,128)} fusion(bf16[2048,256]{0,1:T(8,128)(2,1)S(1)} %copy-done.8, s32[2048,256]{1,0:T(8,128)S(1)} %copy-done, f32[3,2048,256]{2,1,0:T(8,128)} %param.7), kind=kOutput, calls=%fused_computation.28 | convolution fusion | flops 2150629376 | bytes 22020096 | tf_op jit(solution)/shard_map/dot_general | solution.py:19
  287.5 54.8 %all-reduce.13.cloned.1.call-done = f32[2048,256]{0,1:T(8,128)} async-done(((f32[2048,256]{0,1:T(8,128)}), f32[2048,256]{0,1:T(8,128)}) %all-reduce.13.cloned.1.call-update) | async-done | bytes 2097168 | tf_op jit(solution)/shard_map/psum | solution.py:28
  342.3 3.6 multiply_subtract_fusion.1
  346.0 0.0 copy-start.1
  346.0 1.3 copy-done.1
  347.3 7.1 %convolution_bitcast_fusion.1 = f32[2048,256]{1,0:T(8,128)} fusion(bf16[2048,2048]{1,0:T(8,128)(2,1)} %param.5, f32[2048,256]{0,1:T(8,128)S(1)} %multiply_subtract_fusion.1), kind=kOutput, calls=%fused_computation.5 | convolution fusion | flops 2148007936 | bytes 12582912 | tf_op jit(solution)/shard_map/dot_general | solution.py:15
  354.4 0.0 all-reduce.15.cloned.1.call-update
  354.4 0.3 all-reduce.17.cloned.1.call-start
  354.7 0.9 copy-done.6
  355.7 9.5 %fusion.16 = f32[2048,2048]{1,0:T(8,128)} fusion(bf16[2048,256]{1,0:T(8,128)(2,1)S(1)} %copy-done.6, bf16[3,2048,256]{2,1,0:T(8,128)(2,1)} %param.8), kind=kOutput, calls=%fused_computation.31 | convolution fusion | flops 2147483648 | bytes 18874368 | tf_op jit(solution)/shard_map/dot_general | solution.py:22
  365.2 10.2 %fusion.13 = f32[2048,2048]{1,0:T(8,128)} fusion(s32[2048,256]{1,0:T(8,128)S(1)} %copy-done, f32[2048,256]{0,1:T(8,128)S(1)} %copy-done.2, f32[3,2048,256]{2,1,0:T(8,128)} %param.7), kind=kOutput, calls=%fused_computation.29 | convolution fusion | flops 2151153664 | bytes 23068672 | tf_op jit(solution)/shard_map/dot_general | solution.py:19
  375.3 39.7 %all-reduce.15.cloned.1.call-done = f32[2048,256]{1,0:T(8,128)} async-done(((f32[2048,256]{1,0:T(8,128)}), f32[2048,256]{1,0:T(8,128)}) %all-reduce.15.cloned.1.call-update) | async-done | bytes 2097168 | tf_op jit(solution)/shard_map/psum | solution.py:20
  415.0 2.9 fusion.5
  417.8 7.1 %convolution_bitcast_fusion = f32[2048,256]{0,1:T(8,128)} fusion(bf16[2048,256]{1,0:T(8,128)(2,1)S(1)} %fusion.5, bf16[2048,2048]{1,0:T(8,128)(2,1)} %param.5), kind=kOutput, calls=%fused_computation.4 | convolution fusion | flops 2147483648 | bytes 11534336 | tf_op jit(solution)/shard_map/dot_general | solution.py:25
  424.9 0.0 all-reduce.17.cloned.1.call-update
  425.0 0.0 copy-start.3
  425.0 34.1 %add_multiply_fusion = f32[2048,2048]{1,0:T(8,128)} fusion(f32[2048,2048]{1,0:T(8,128)} %fusion.13, f32[2048,2048]{1,0:T(8,128)} %fusion.16, f32[2048,2048]{1,0:T(8,128)} %fusion.11, f32[2048,2048]{1,0:T(8,128)} %fusion.9, f32[2048,2048]{1,0:T(8,128)} %fusion.18, bf16[2048,256]{1,0:T(8,128)(2,1)S(1)} %fusion.5, bf16[3,2048,256]{2,1,0:T(8,128)(2,1)} %param.8), kind=kOutput, calls=%fused_computation | convolution fusion | flops 2172649472 | bytes 102760448 | tf_op jit(solution)/shard_map/dot_general | solution.py:22
  459.1 51.8 %all-reduce.17.cloned.1.call-done = f32[2048,256]{0,1:T(8,128)} async-done(((f32[2048,256]{0,1:T(8,128)}), f32[2048,256]{0,1:T(8,128)}) %all-reduce.17.cloned.1.call-update) | async-done | bytes 2097168 | tf_op jit(solution)/shard_map/psum | solution.py:28
  510.8 3.2 multiply_subtract_fusion
  514.1 2.9 copy.10
  (8 shorter events, 0.0 us)
Async XLA Ops:
  7.2 72.0 %all-reduce.7.cloned.1.call-start = ((), (), s32[]{:S(2)}) async-start(), calls=%async_computation | async-start | bytes 4194304 | tf_op jit(solution)/shard_map/psum | solution.py:20
  14.9 160.1 %all-reduce.9.cloned.1.call-start = ((), (), s32[]{:S(2)}) async-start(), calls=%async_computation.1 | async-start | bytes 4194304 | tf_op jit(solution)/shard_map/psum | solution.py:28
  89.1 156.5 %all-reduce.11.cloned.1.call-start = ((), (), s32[]{:S(2)}) async-start(), calls=%async_computation.2 | async-start | bytes 4194304 | tf_op jit(solution)/shard_map/psum | solution.py:20
  91.1 85.8 %copy-start.4 = (f32[2048,256]{0,1:T(8,128)}, f32[2048,256]{0,1:T(8,128)S(1)}, u32[]{:S(2)}) copy-start(f32[2048,256]{0,1:T(8,128)S(1)} %copy.7) | copy-start | bytes 6291460
  176.9 1.0 copy-start.7
  185.0 157.3 %all-reduce.13.cloned.1.call-start = ((), (), s32[]{:S(2)}) async-start(), calls=%async_computation.3 | async-start | bytes 4194304 | tf_op jit(solution)/shard_map/psum | solution.py:28
  248.4 1.0 copy-start.5
  256.4 1.6 copy-start
  256.5 158.5 %all-reduce.15.cloned.1.call-start = ((), (), s32[]{:S(2)}) async-start(), calls=%async_computation.4 | async-start | bytes 4194304 | tf_op jit(solution)/shard_map/psum | solution.py:20
  268.4 9.4 %copy-start.8 = (bf16[2048,256]{0,1:T(8,128)(2,1)S(1)}, bf16[2048,256]{0,1:T(8,128)(2,1)}, u32[]{:S(2)}) copy-start(bf16[2048,256]{0,1:T(8,128)(2,1)} %copy-done.7) | copy-start | bytes 3145732
  346.0 1.3 copy-start.1
  354.4 1.2 copy-start.6
  354.4 156.4 %all-reduce.17.cloned.1.call-start = ((), (), s32[]{:S(2)}) async-start(), calls=%async_computation.5 | async-start | bytes 4194304 | tf_op jit(solution)/shard_map/psum | solution.py:28
  355.6 9.5 %copy-start.2 = (f32[2048,256]{0,1:T(8,128)S(1)}, f32[2048,256]{0,1:T(8,128)}, u32[]{:S(2)}) copy-start(f32[2048,256]{0,1:T(8,128)} %copy-done.1) | copy-start | bytes 6291460
  425.0 85.9 %copy-start.3 = (f32[2048,256]{0,1:T(8,128)S(1)}, f32[2048,256]{0,1:T(8,128)}, u32[]{:S(2)}) copy-start(f32[2048,256]{0,1:T(8,128)} %copy-done.1) | copy-start | bytes 6291460
Sparse Core Ops, SparseCore 0:
  15.0 64.0 all-reduce.6
  89.2 85.7 all-reduce.8
  185.1 60.3 all-reduce.10
  256.6 85.6 all-reduce.12
  354.6 60.3 all-reduce.14
  425.1 85.7 all-reduce.16
where the time goes:
time: 524 us
  waiting for transfers between devices  355 us (68%)
  matrix products  126 us (24%)
  other arithmetic  17.3 us (3%)
  between operations  14.2 us (3%)
  local copies, waits for them, and re-layouts  10.4 us (2%)
    psum x3, waiting for transfers between devices, shards(): hessian_term = lax.psum(local_hess, 'row')  190 us
    psum x3, waiting for transfers between devices, shards(): product = lax.psum(local_sum, 'inst')  164 us
    dot_general x3, matrix products, shards(): jnp.dot(weighted, saved_coefficients[step].T, preferred_element_type=jnp....  53 us
    dot_general x3, matrix products, shards(): jnp.dot(residual, adjoint_low.T, preferred_element_type=jnp.float32)  30.2 us
    dot_general x3, matrix products, shards(): local_sum = jnp.dot(design, adjoint_low, preferred_element_type=jnp.float32)  21.9 us
    dot_general x3, matrix products, shards(): lax.dot_general(design, weighted, (((0,), (0,)), ((), ())), preferred_ele...  21.2 us
  transfers between devices with their start and end apart: 6, of which 6 were waited for; matrix products, arithmetic and copies ran while one was open for 16% of the time, Pallas kernels for 0%

commit v1 on v0

v1 whole, which is shorter than its diff:
```python
import functools

import jax
import jax.numpy as jnp
from jax import lax
from jax.experimental import pallas as pl
from jax.experimental.pallas import tpu as pltpu
from jax.sharding import PartitionSpec as P

RATE = 2.0
CHAINS = 2
PIECES = 2
F32 = jnp.float32
BF16 = jnp.bfloat16
VMEM = pl.BlockSpec(memory_space=pltpu.VMEM)
SMEM = pl.BlockSpec(memory_space=pltpu.SMEM)


def cost(flops, nbytes):
    return pl.CostEstimate(flops=flops, bytes_accessed=nbytes, transcendentals=0)


def forward_kernel(core, z, low, keep, send):
    half = keep.shape[0]
    own = pl.multiple_of(core[0] * half, half)
    other = pl.multiple_of((1 - core[0]) * half, half)
    send[...] = jnp.dot(z[pl.ds(other, half), :], low[...], preferred_element_type=F32).astype(BF16)
    keep[...] = jnp.dot(z[pl.ds(own, half), :], low[...], preferred_element_type=F32)


def forward(core, z, low):
    half, cols = z.shape[0] // 2, low.shape[1]
    return pl.pallas_call(
        forward_kernel,
        in_specs=[SMEM, VMEM, VMEM],
        out_specs=[VMEM, VMEM],
        out_shape=[jax.ShapeDtypeStruct((half, cols), F32), jax.ShapeDtypeStruct((half, cols), BF16)],
        compiler_params=pltpu.CompilerParams(vmem_limit_bytes=14 << 20),
        cost_estimate=cost(2 * z.shape[0] * z.shape[1] * 256, 1 << 20),
        name="forward",
    )(core, z, low)


def backward_kernel(piece, core, z, w_own, w_other, out):
    half, width = w_own.shape[0], out.shape[0]
    own = pl.multiple_of(core[0] * half, half)
    other = pl.multiple_of((1 - core[0]) * half, half)
    cols = pl.ds(piece * width, width)
    dims = (((0,), (0,)), ((), ()))
    total = lax.dot_general(w_own[...], z[pl.ds(own, half), cols], dims, preferred_element_type=F32)
    total += lax.dot_general(w_other[...], z[pl.ds(other, half), cols], dims, preferred_element_type=F32)
    out[...] = total.T.astype(BF16)


def backward(core, z, w_own, w_other, piece, pieces):
    width = z.shape[1] // pieces
    return pl.pallas_call(
        functools.partial(backward_kernel, piece),
        in_specs=[SMEM, VMEM, VMEM, VMEM],
        out_specs=VMEM,
        out_shape=jax.ShapeDtypeStruct((width, w_own.shape[1]), BF16),
        compiler_params=pltpu.CompilerParams(vmem_limit_bytes=14 << 20),
        cost_estimate=cost(2 * z.shape[0] * width * 256, 1 << 20),
        name="backward",
    )(core, z, w_own, w_other)


def outer_kernel(count, *refs):
    left, right, out = refs[:count], refs[count : 2 * count], refs[2 * count]
    dims = (((1,), (1,)), ((), ()))
    total = lax.dot_general(left[0][...], right[0][...], dims, preferred_element_type=F32)
    for a, b in zip(left[1:], right[1:]):
        total += lax.dot_general(a[...], b[...], dims, preferred_element_type=F32)
    out[...] = -RATE * total


def outer(left, right):
    rows, depth = left[0].shape
    cols = right[0].shape[0]
    block = min(256, rows)
    return pl.pallas_call(
        functools.partial(outer_kernel, len(left)),
        grid=(rows // block,),
        in_specs=[pl.BlockSpec((block, depth), lambda i: (i, 0)) for _ in left] + [VMEM for _ in right],
        out_specs=pl.BlockSpec((block, cols), lambda i: (i, 0)),
        out_shape=jax.ShapeDtypeStruct((rows, cols), F32),
        compiler_params=pltpu.CompilerParams(vmem_limit_bytes=30 << 20),
        cost_estimate=cost(2 * rows * cols * depth * len(left), rows * cols * 4),
        name="outer",
    )(*left, *right)


def sum_inst(keep, send, count):
    bits = [1 << b for b in range(1, count.bit_length() - 1)]
    total = keep + lax.ppermute(send, "inst", [(i, i ^ 1) for i in range(count)]).astype(F32)
    for step in range(len(bits)):
        order = (bits[step], bits[(step + 1) % len(bits)])
        pairs = [(i, i ^ order[i & 1]) for i in range(count)]
        total = total + lax.ppermute(total.astype(BF16), "inst", pairs).astype(F32)
    return total


def sum_row(parts, place, count):
    middle = count // 2
    for hop in range(middle - 1):
        pairs = [(hop, hop + 1), (count - 1 - hop, count - 2 - hop)]
        parts = [
            (p.astype(F32) + lax.ppermute(p, "row", pairs).astype(F32)).astype(BF16) for p in parts
        ]
    pairs = [(middle - 1, middle), (middle, middle - 1)]
    parts = [(p.astype(F32) + lax.ppermute(p, "row", pairs).astype(F32)).astype(BF16) for p in parts]
    for hop in range(middle - 1, 0, -1):
        pairs = [(hop, hop - 1), (count - 1 - hop, count - hop)]
        takes = (place == hop - 1) | (place == count - hop)
        parts = [jnp.where(takes, lax.ppermute(p, "row", pairs), p) for p in parts]
    return parts


def shards(rows_count, inst_count, design, labels, saved_logits, saved_coefficients, cotangent):
    steps, rows, depth = saved_logits.shape
    half, cols = rows // 2, depth // CHAINS
    width = design.shape[1] // PIECES
    core = lax.axis_index("inst") % 2
    place = lax.axis_index("row")
    core_ref = core.astype(jnp.int32).reshape(1)
    swap = [(i, i ^ 1) for i in range(inst_count)]
    targets = labels.astype(F32)
    adjoint = [
        [cotangent[p * width : (p + 1) * width, c * cols : (c + 1) * cols] for p in range(PIECES)]
        for c in range(CHAINS)
    ]
    left, right = [], []
    for step in range(steps - 1, -1, -1):
        residual = (jax.nn.sigmoid(saved_logits[step]) - targets).astype(BF16)
        lows, weights = [], []
        for c in range(CHAINS):
            low = jnp.concatenate([p.astype(BF16) for p in adjoint[c]], axis=0)
            keep, send = forward(core_ref, design, low)
            product = sum_inst(keep, send, inst_count)
            logits = lax.dynamic_slice(
                saved_logits, (step, core * half, c * cols), (1, half, cols)
            )[0]
            probability = jax.nn.sigmoid(logits)
            w_own = (probability * (1.0 - probability) * product).astype(BF16)
            w_other = lax.ppermute(w_own, "inst", swap)
            hessian = [
                backward(core_ref, design, w_own, w_other, p, PIECES) for p in range(PIECES)
            ]
            hessian = sum_row(hessian, place, rows_count)
            adjoint[c] = [a - RATE * h.astype(F32) for a, h in zip(adjoint[c], hessian)]
            lows.append(low)
            weights.append(
                jnp.where(
                    core == 0,
                    jnp.concatenate([w_own, w_other], axis=0),
                    jnp.concatenate([w_other, w_own], axis=0),
                )
            )
        left += [residual, jnp.concatenate(weights, axis=1)]
        right += [jnp.concatenate(lows, axis=1), saved_coefficients[step]]
    first = jnp.concatenate([jnp.concatenate(a, axis=0) for a in adjoint], axis=1)
    return first, outer(left, right)


def solution(mesh):
    placed = (
        P("row", "inst"),
        P("row", None),
        P(None, "row", None),
        P(None, "inst", None),
        P("inst", None),
    )
    return jax.shard_map(
        functools.partial(shards, mesh.shape["row"], mesh.shape["inst"]),
        mesh=mesh,
        in_specs=placed,
        out_specs=(P("inst", None), P("row", "inst")),
        check_vma=False,
    )
```

time: 524 us -> 268 us (0.51)
  waiting for transfers between devices: 355 us -> 121 us
  matrix products: 126 us -> 0 us
  starting transfers between devices: 0.65 us -> 66.9 us
  Pallas kernels: 0 us -> 39.7 us
  between operations: 14.2 us -> 2.07 us
  local copies, waits for them, and re-layouts: 10.4 us -> 18.7 us
    psum x6 -> x0, waiting for transfers between devices: 355 us -> none  [the longest x3 190 us: shards(): hessian_term = lax.psum(local_hess, 'row')]
    dot_general x12 -> x0, matrix products: 126 us -> none  [the longest x3 53 us: shards(): jnp.dot(weighted, saved_coefficients[step].T, preferred_element_type=jnp....]
    ppermute x0 -> x60, waiting for transfers between devices: none -> 121 us  [the longest x12 67.7 us: sum_row(): parts = [jnp.where(takes, lax.ppermute(p, 'row', pairs), p) for p in parts]]
    ppermute x0 -> x60, starting transfers between devices: none -> 66.9 us  [the longest x24 27 us: sum_row(): lax.ppermute(p, 'row', pairs).astype(F32)]
    pallas_call x0 -> x19, Pallas kernels: none -> 39.7 us  [the longest x1 16 us: outer(): pl.pallas_call(functools.partial(outer_kernel, len(left)), grid=(rows //...]
    unnamed x20 -> x86, local copies, waits for them, and re-layouts: 10.4 us -> 15.3 us
    convert_element_type x4 -> x43, other arithmetic: 10.5 us -> 13.2 us  [the longest x3 3.91 us: shards(): w_own = (probability * (1.0 - probability) * product).astype(BF16)]
  transfers between devices with their start and end apart: 6 -> 60, of which waited for: 6 -> 33; matrix products, arithmetic and copies ran while one was open for 16% -> 4% of each run, Pallas kernels for 0% -> 13%
where the time goes in v1:
time: 268 us; the launch traced here: 267 us
  waiting for transfers between devices  121 us (45%)
  starting transfers between devices  66.9 us (25%)
  Pallas kernels  39.7 us (15%)
  local copies, waits for them, and re-layouts  18.7 us (7%)
  other arithmetic  18.4 us (7%)
    ppermute x12, waiting for transfers between devices, sum_row(): parts = [jnp.where(takes, lax.ppermute(p, 'row', pairs), p) for p in parts]  67.7 us
    ppermute x24, waiting for transfers between devices, sum_row(): lax.ppermute(p, 'row', pairs).astype(F32)  27.9 us
    ppermute x24, starting transfers between devices, sum_row(): lax.ppermute(p, 'row', pairs).astype(F32)  27 us
    ppermute x12, waiting for transfers between devices, sum_inst(): total = total + lax.ppermute(total.astype(BF16), 'inst', pairs).astype(F32)  23.4 us
    ppermute x12, starting transfers between devices, sum_inst(): total = total + lax.ppermute(total.astype(BF16), 'inst', pairs).astype(F32)  20.8 us
    pallas_call x1, Pallas kernels, outer(): pl.pallas_call(functools.partial(outer_kernel, len(left)), grid=(rows //...  16 us
    ppermute x12, starting transfers between devices, sum_row(): parts = [jnp.where(takes, lax.ppermute(p, 'row', pairs), p) for p in parts]  15.9 us
    unnamed x86, local copies, waits for them, and re-layouts  15.3 us
  transfers between devices with their start and end apart: 60, of which 33 were waited for; matrix products, arithmetic and copies ran while one was open for 4% of the time, Pallas kernels for 13%

profile of v1, /device:TPU:0, one launch (start us, length us, event | category | flops | bytes accessed | tf_op | source)
XLA Modules:
  0.0 267.2 jit_solution(226688776569029554)
XLA Ops:
  0.6 1.7 fusion.35
  3.1 3.4 %copy-done = bf16[2048,2048]{1,0:T(8,128)(2,1)S(1)} copy-done((bf16[2048,2048]{1,0:T(8,128)(2,1)S(1)}, bf16[2048,2048]{1,0:T(8,128)(2,1)}, u32[]{:S(2)}) %copy-start) | copy-done | bytes 8388632
  6.5 2.3 forward.6
  9.4 2.3 forward.9
  11.9 3.0 %collective-permute-start.1 = (bf16[1024,128]{1,0:T(8,128)(2,1)S(1)}, bf16[1024,128]{1,0:T(8,128)(2,1)S(1)}, u32[]{:S(2)}, u32[]{:S(2)}) collective-permute-start(bf16[1024,128]{1,0:T(8,128)(2,1)S(1)} %fusion.15), channel_id=1, source_target_pairs={{0,2},{1,5},{2,0},{3,7},{4,6},{5,1},{6,4},{7,3},{8,10},{9,13},{10,... | collective-permute-start | bytes 786440 | tf_op jit(solution)/shard_map/ppermute | solution.py:99
  16.0 3.2 %collective-permute-done.1 = bf16[1024,128]{1,0:T(8,128)(2,1)S(1)} collective-permute-done((bf16[1024,128]{1,0:T(8,128)(2,1)S(1)}, bf16[1024,128]{1,0:T(8,128)(2,1)S(1)}, u32[]{:S(2)}, u32[]{:S(2)}) %collective-permute-start.1) | collective-permute-done | bytes 262176 | tf_op jit(solution)/shard_map/ppermute | solution.py:99
  19.3 2.1 collective-permute-start.2
  22.6 2.4 collective-permute-start.32
  25.8 3.6 %collective-permute-done.32 = bf16[1024,128]{1,0:T(8,128)(2,1)S(1)} collective-permute-done((bf16[1024,128]{1,0:T(8,128)(2,1)S(1)}, bf16[1024,128]{1,0:T(8,128)(2,1)S(1)}, u32[]{:S(2)}, u32[]{:S(2)}) %collective-permute-start.32) | collective-permute-done | bytes 262176 | tf_op jit(solution)/shard_map/ppermute | solution.py:99
  29.4 1.7 fusion.4
  32.7 3.4 %copy-done.1 = bf16[2048,2048]{1,0:T(8,128)(2,1)S(1)} copy-done((bf16[2048,2048]{1,0:T(8,128)(2,1)S(1)}, bf16[2048,2048]{1,0:T(8,128)(2,1)}, u32[]{:S(2)}) %copy-start.1) | copy-done | bytes 8388632
  36.9 4.0 %collective-permute-start.4 = (bf16[1024,128]{1,0:T(8,128)(2,1)S(1)}, bf16[1024,128]{1,0:T(8,128)(2,1)S(1)}, u32[]{:S(2)}, u32[]{:S(2)}) collective-permute-start(bf16[1024,128]{1,0:T(8,128)(2,1)S(1)} %backward.12), channel_id=1, source_target_pairs={{0,8},{24,16},{1,9},{25,17},{2,10},{26,18},{3,11},{27,19},{4,12},{... | collective-permute-start | bytes 786440 | tf_op jit(solution)/shard_map/ppermute | solution.py:108
  48.3 4.9 %collective-permute-done.7 = bf16[1024,128]{1,0:T(8,128)(2,1)S(1)} collective-permute-done((bf16[1024,128]{1,0:T(8,128)(2,1)S(1)}, bf16[1024,128]{1,0:T(8,128)(2,1)S(1)}, u32[]{:S(2)}, u32[]{:S(2)}) %collective-permute-start.7) | collective-permute-done | bytes 262176 | tf_op jit(solution)/shard_map/ppermute | solution.py:108
  53.9 4.9 %collective-permute-done.34 = bf16[1024,128]{1,0:T(8,128)(2,1)S(1)} collective-permute-done((bf16[1024,128]{1,0:T(8,128)(2,1)S(1)}, bf16[1024,128]{1,0:T(8,128)(2,1)S(1)}, u32[]{:S(2)}, u32[]{:S(2)}) %collective-permute-start.34) | collective-permute-done | bytes 262176 | tf_op jit(solution)/shard_map/ppermute | solution.py:108
  59.5 4.1 %collective-permute-done.37 = bf16[1024,128]{1,0:T(8,128)(2,1)S(1)} collective-permute-done((bf16[1024,128]{1,0:T(8,128)(2,1)S(1)}, bf16[1024,128]{1,0:T(8,128)(2,1)S(1)}, u32[]{:S(2)}, u32[]{:S(2)}) %collective-permute-start.37) | collective-permute-done | bytes 262176 | tf_op jit(solution)/shard_map/ppermute | solution.py:108
  70.1 8.1 %collective-permute-done.6 = bf16[1024,128]{1,0:T(8,128)(2,1)S(1)} collective-permute-done((bf16[1024,128]{1,0:T(8,128)(2,1)S(1)}, bf16[1024,128]{1,0:T(8,128)(2,1)S(1)}, u32[]{:S(2)}, u32[]{:S(2)}) %collective-permute-start.6) | collective-permute-done | bytes 262176 | tf_op jit(solution)/shard_map/ppermute | solution.py:115
  78.2 5.6 %collective-permute-done.9 = bf16[1024,128]{1,0:T(8,128)(2,1)S(1)} collective-permute-done((bf16[1024,128]{1,0:T(8,128)(2,1)S(1)}, bf16[1024,128]{1,0:T(8,128)(2,1)S(1)}, u32[]{:S(2)}, u32[]{:S(2)}) %collective-permute-start.9) | collective-permute-done | bytes 262176 | tf_op jit(solution)/shard_map/ppermute | solution.py:115
  83.8 5.6 %collective-permute-done.36 = bf16[1024,128]{1,0:T(8,128)(2,1)S(1)} collective-permute-done((bf16[1024,128]{1,0:T(8,128)(2,1)S(1)}, bf16[1024,128]{1,0:T(8,128)(2,1)S(1)}, u32[]{:S(2)}, u32[]{:S(2)}) %collective-permute-start.36) | collective-permute-done | bytes 262176 | tf_op jit(solution)/shard_map/ppermute | solution.py:115
  89.5 4.0 %collective-permute-done.39 = bf16[1024,128]{1,0:T(8,128)(2,1)} collective-permute-done((bf16[1024,128]{1,0:T(8,128)(2,1)S(1)}, bf16[1024,128]{1,0:T(8,128)(2,1)}, u32[]{:S(2)}, u32[]{:S(2)}) %collective-permute-start.39) | collective-permute-done | bytes 262176 | tf_op jit(solution)/shard_map/ppermute | solution.py:115
  93.5 2.0 fusion.31
  96.3 3.4 %copy-done.2 = bf16[2048,2048]{1,0:T(8,128)(2,1)S(1)} copy-done((bf16[2048,2048]{1,0:T(8,128)(2,1)S(1)}, bf16[2048,2048]{1,0:T(8,128)(2,1)}, u32[]{:S(2)}) %copy-start.2) | copy-done | bytes 8388632
  99.6 2.3 forward.7
  102.1 2.3 forward.10
  107.8 2.9 %fusion = (bf16[2048,256]{1,0:T(8,128)(2,1)}, bf16[2048,256]{1,0:T(8,128)(2,1)}, bf16[2048,256]{1,0:T(8,128)(2,1)}) fusion(f32[3,2048,256]{2,1,0:T(8,128)S(1)} %bitcast.34, s32[2048,256]{1,0:T(8,128)S(1)} %copy-done.38), kind=kLoop, calls=%fused_computation.2 | loop fusion | flops 8388608 | bytes 11534336 | tf_op jit(solution)/shard_map/convert_element_type | solution.py:134
  111.6 1.6 collective-permute-start.12
  113.2 1.8 collective-permute-done.41
  115.1 1.7 collective-permute-start.42
  116.8 1.8 slice_bitcast_fusion
  118.6 3.0 %collective-permute-done.42 = bf16[1024,128]{1,0:T(8,128)(2,1)S(1)} collective-permute-done((bf16[1024,128]{1,0:T(8,128)(2,1)S(1)}, bf16[1024,128]{1,0:T(8,128)(2,1)S(1)}, u32[]{:S(2)}, u32[]{:S(2)}) %collective-permute-start.42) | collective-permute-done | bytes 262176 | tf_op jit(solution)/shard_map/ppermute | solution.py:99
  123.7 3.4 %copy-done.3 = bf16[2048,2048]{1,0:T(8,128)(2,1)S(1)} copy-done((bf16[2048,2048]{1,0:T(8,128)(2,1)S(1)}, bf16[2048,2048]{1,0:T(8,128)(2,1)}, u32[]{:S(2)}) %copy-start.3) | copy-done | bytes 8388632
  136.5 4.8 %collective-permute-done.17 = bf16[1024,128]{1,0:T(8,128)(2,1)S(1)} collective-permute-done((bf16[1024,128]{1,0:T(8,128)(2,1)S(1)}, bf16[1024,128]{1,0:T(8,128)(2,1)S(1)}, u32[]{:S(2)}, u32[]{:S(2)}) %collective-permute-start.17) | collective-permute-done | bytes 262176 | tf_op jit(solution)/shard_map/ppermute | solution.py:108
  142.2 4.9 %collective-permute-done.44 = bf16[1024,128]{1,0:T(8,128)(2,1)S(1)} collective-permute-done((bf16[1024,128]{1,0:T(8,128)(2,1)S(1)}, bf16[1024,128]{1,0:T(8,128)(2,1)S(1)}, u32[]{:S(2)}, u32[]{:S(2)}) %collective-permute-start.44) | collective-permute-done | bytes 262176 | tf_op jit(solution)/shard_map/ppermute | solution.py:108
  147.9 4.2 %collective-permute-done.47 = bf16[1024,128]{1,0:T(8,128)(2,1)S(1)} collective-permute-done((bf16[1024,128]{1,0:T(8,128)(2,1)S(1)}, bf16[1024,128]{1,0:T(8,128)(2,1)S(1)}, u32[]{:S(2)}, u32[]{:S(2)}) %collective-permute-start.47) | collective-permute-done | bytes 262176 | tf_op jit(solution)/shard_map/ppermute | solution.py:108
  158.8 6.8 %collective-permute-done.16 = bf16[1024,128]{1,0:T(8,128)(2,1)S(1)} collective-permute-done((bf16[1024,128]{1,0:T(8,128)(2,1)S(1)}, bf16[1024,128]{1,0:T(8,128)(2,1)S(1)}, u32[]{:S(2)}, u32[]{:S(2)}) %collective-permute-start.16) | collective-permute-done | bytes 262176 | tf_op jit(solution)/shard_map/ppermute | solution.py:115
  165.6 5.6 %collective-permute-done.19 = bf16[1024,128]{1,0:T(8,128)(2,1)S(1)} collective-permute-done((bf16[1024,128]{1,0:T(8,128)(2,1)S(1)}, bf16[1024,128]{1,0:T(8,128)(2,1)S(1)}, u32[]{:S(2)}, u32[]{:S(2)}) %collective-permute-start.19) | collective-permute-done | bytes 262176 | tf_op jit(solution)/shard_map/ppermute | solution.py:115
  171.3 5.6 %collective-permute-done.46 = bf16[1024,128]{1,0:T(8,128)(2,1)S(1)} collective-permute-done((bf16[1024,128]{1,0:T(8,128)(2,1)S(1)}, bf16[1024,128]{1,0:T(8,128)(2,1)S(1)}, u32[]{:S(2)}, u32[]{:S(2)}) %collective-permute-start.46) | collective-permute-done | bytes 262176 | tf_op jit(solution)/shard_map/ppermute | solution.py:115
  177.6 2.3 forward.8
  182.3 2.3 forward.11
  188.0 3.3 %collective-permute-done.21 = bf16[1024,128]{1,0:T(8,128)(2,1)S(1)} collective-permute-done((bf16[1024,128]{1,0:T(8,128)(2,1)S(1)}, bf16[1024,128]{1,0:T(8,128)(2,1)S(1)}, u32[]{:S(2)}, u32[]{:S(2)}) %collective-permute-start.21) | collective-permute-done | bytes 262176 | tf_op jit(solution)/shard_map/ppermute | solution.py:99
  191.5 1.7 collective-permute-start.22
  194.7 1.7 collective-permute-start.52
  198.0 3.1 %collective-permute-done.52 = bf16[1024,128]{1,0:T(8,128)(2,1)S(1)} collective-permute-done((bf16[1024,128]{1,0:T(8,128)(2,1)S(1)}, bf16[1024,128]{1,0:T(8,128)(2,1)S(1)}, u32[]{:S(2)}, u32[]{:S(2)}) %collective-permute-start.52) | collective-permute-done | bytes 262176 | tf_op jit(solution)/shard_map/ppermute | solution.py:99
  201.1 1.7 fusion.8
  214.0 16.0 %outer.1 = f32[2048,2048]{1,0:T(8,128)} custom-call(bf16[2048,256]{1,0:T(8,128)(2,1)S(1)} %copy-done.8, bf16[2048,256]{1,0:T(8,128)(2,1)S(1)} %pad_maximum_fusion.refs_1_, bf16[2048,256]{1,0:T(8,128)(2,1)S(1)} %copy-done.9, bf16[2048,256]{1,0:T(8,128)(2,1)S(1)} %pad_maximum_fusion.1.refs_3_, bf16[2048,256]{1,0:T(8,128)(2,1)S(1)} %copy-done.7, ...), custom_call_target="tpu_custom_call" | custom-call | flops 12884901888 | bytes 16777216 | tf_op jit(solution)/shard_map/outer/pallas_call | solution.py:81
  238.6 10.2 %collective-permute-done.26 = bf16[1024,128]{1,0:T(8,128)(2,1)S(1)} collective-permute-done((bf16[1024,128]{1,0:T(8,128)(2,1)S(1)}, bf16[1024,128]{1,0:T(8,128)(2,1)S(1)}, u32[]{:S(2)}, u32[]{:S(2)}) %collective-permute-start.26) | collective-permute-done | bytes 262176 | tf_op jit(solution)/shard_map/ppermute | solution.py:115
  248.8 5.6 %collective-permute-done.29 = bf16[1024,128]{1,0:T(8,128)(2,1)S(1)} collective-permute-done((bf16[1024,128]{1,0:T(8,128)(2,1)S(1)}, bf16[1024,128]{1,0:T(8,128)(2,1)S(1)}, u32[]{:S(2)}, u32[]{:S(2)}) %collective-permute-start.29) | collective-permute-done | bytes 262176 | tf_op jit(solution)/shard_map/ppermute | solution.py:115
  255.0 5.1 %collective-permute-done.56 = bf16[1024,128]{1,0:T(8,128)(2,1)S(1)} collective-permute-done((bf16[1024,128]{1,0:T(8,128)(2,1)S(1)}, bf16[1024,128]{1,0:T(8,128)(2,1)S(1)}, u32[]{:S(2)}, u32[]{:S(2)}) %collective-permute-start.56) | collective-permute-done | bytes 262176 | tf_op jit(solution)/shard_map/ppermute | solution.py:115
  260.1 4.2 %collective-permute-done.59 = bf16[1024,128]{1,0:T(8,128)(2,1)S(1)} collective-permute-done((bf16[1024,128]{1,0:T(8,128)(2,1)S(1)}, bf16[1024,128]{1,0:T(8,128)(2,1)S(1)}, u32[]{:S(2)}, u32[]{:S(2)}) %collective-permute-start.59) | collective-permute-done | bytes 262176 | tf_op jit(solution)/shard_map/ppermute | solution.py:115
  (244 shorter events, 79.7 us)
Async XLA Ops:
  11.9 7.4 %collective-permute-start.1 = (bf16[1024,128]{1,0:T(8,128)(2,1)S(1)}, bf16[1024,128]{1,0:T(8,128)(2,1)S(1)}, u32[]{:S(2)}, u32[]{:S(2)}) collective-permute-start(bf16[1024,128]{1,0:T(8,128)(2,1)S(1)} %fusion.15), channel_id=1, source_target_pairs={{0,2},{1,5},{2,0},{3,7},{4,6},{5,1},{6,4},{7,3},{8,10},{9,13},{10,... | collective-permute-start | bytes 786440 | tf_op jit(solution)/shard_map/ppermute | solution.py:99
  14.9 7.6 %collective-permute-start.31 = (bf16[1024,128]{1,0:T(8,128)(2,1)S(1)}, bf16[1024,128]{1,0:T(8,128)(2,1)S(1)}, u32[]{:S(2)}, u32[]{:S(2)}) collective-permute-start(bf16[1024,128]{1,0:T(8,128)(2,1)S(1)} %fusion.18), channel_id=1, source_target_pairs={{0,2},{1,5},{2,0},{3,7},{4,6},{5,1},{6,4},{7,3},{8,10},{9,13},{10,... | collective-permute-start | bytes 786440 | tf_op jit(solution)/shard_map/ppermute | solution.py:99
  19.3 6.5 %collective-permute-start.2 = (bf16[1024,128]{1,0:T(8,128)(2,1)S(1)}, bf16[1024,128]{1,0:T(8,128)(2,1)S(1)}, u32[]{:S(2)}, u32[]{:S(2)}) collective-permute-start(bf16[1024,128]{1,0:T(8,128)(2,1)S(1)} %fusion.25), channel_id=1, source_target_pairs={{0,4},{1,3},{2,6},{3,1},{4,0},{5,7},{6,2},{7,5},{8,12},{9,11},{10,... | collective-permute-start | bytes 786440 | tf_op jit(solution)/shard_map/ppermute | solution.py:99
  22.6 6.8 %collective-permute-start.32 = (bf16[1024,128]{1,0:T(8,128)(2,1)S(1)}, bf16[1024,128]{1,0:T(8,128)(2,1)S(1)}, u32[]{:S(2)}, u32[]{:S(2)}) collective-permute-start(bf16[1024,128]{1,0:T(8,128)(2,1)S(1)} %fusion.28), channel_id=1, source_target_pairs={{0,4},{1,3},{2,6},{3,1},{4,0},{5,7},{6,2},{7,5},{8,12},{9,11},{10,... | collective-permute-start | bytes 786440 | tf_op jit(solution)/shard_map/ppermute | solution.py:99
  31.2 11.9 %collective-permute-start.33 = (bf16[1024,128]{1,0:T(8,128)(2,1)S(1)}, bf16[1024,128]{1,0:T(8,128)(2,1)S(1)}, u32[]{:S(2)}, u32[]{:S(2)}) collective-permute-start(bf16[1024,128]{1,0:T(8,128)(2,1)S(1)} %get-tuple-element.34.w_own), channel_id=1, source_target_pairs={{0,1},{1,0},{2,3},{3,2},{4,5},{5,4},{6,7},{7,6},{8,9},{9,8},{10,11... | collective-permute-start | bytes 786440 | tf_op jit(solution)/shard_map/ppermute | solution.py:145
  36.9 10.6 %collective-permute-start.4 = (bf16[1024,128]{1,0:T(8,128)(2,1)S(1)}, bf16[1024,128]{1,0:T(8,128)(2,1)S(1)}, u32[]{:S(2)}, u32[]{:S(2)}) collective-permute-start(bf16[1024,128]{1,0:T(8,128)(2,1)S(1)} %backward.12), channel_id=1, source_target_pairs={{0,8},{24,16},{1,9},{25,17},{2,10},{26,18},{3,11},{27,19},{4,12},{... | collective-permute-start | bytes 786440 | tf_op jit(solution)/shard_map/ppermute | solution.py:108
  41.7 11.4 %collective-permute-start.7 = (bf16[1024,128]{1,0:T(8,128)(2,1)S(1)}, bf16[1024,128]{1,0:T(8,128)(2,1)S(1)}, u32[]{:S(2)}, u32[]{:S(2)}) collective-permute-start(bf16[1024,128]{1,0:T(8,128)(2,1)S(1)} %backward.13), channel_id=1, source_target_pairs={{0,8},{24,16},{1,9},{25,17},{2,10},{26,18},{3,11},{27,19},{4,12},{... | collective-permute-start | bytes 786440 | tf_op jit(solution)/shard_map/ppermute | solution.py:108
  43.9 14.9 %collective-permute-start.34 = (bf16[1024,128]{1,0:T(8,128)(2,1)S(1)}, bf16[1024,128]{1,0:T(8,128)(2,1)S(1)}, u32[]{:S(2)}, u32[]{:S(2)}) collective-permute-start(bf16[1024,128]{1,0:T(8,128)(2,1)S(1)} %backward.18), channel_id=1, source_target_pairs={{0,8},{24,16},{1,9},{25,17},{2,10},{26,18},{3,11},{27,19},{4,12},{... | collective-permute-start | bytes 786440 | tf_op jit(solution)/shard_map/ppermute | solution.py:108
  46.0 17.6 %collective-permute-start.37 = (bf16[1024,128]{1,0:T(8,128)(2,1)S(1)}, bf16[1024,128]{1,0:T(8,128)(2,1)S(1)}, u32[]{:S(2)}, u32[]{:S(2)}) collective-permute-start(bf16[1024,128]{1,0:T(8,128)(2,1)S(1)} %backward.19), channel_id=1, source_target_pairs={{0,8},{24,16},{1,9},{25,17},{2,10},{26,18},{3,11},{27,19},{4,12},{... | collective-permute-start | bytes 786440 | tf_op jit(solution)/shard_map/ppermute | solution.py:108
  47.6 16.7 %collective-permute-start.5 = (bf16[1024,128]{1,0:T(8,128)(2,1)S(1)}, bf16[1024,128]{1,0:T(8,128)(2,1)S(1)}, u32[]{:S(2)}, u32[]{:S(2)}) collective-permute-start(bf16[1024,128]{1,0:T(8,128)(2,1)S(1)} %add_convert_fusion.23), channel_id=1, source_target_pairs={{8,16},{16,8},{9,17},{17,9},{10,18},{18,10},{11,19},{19,11},{12,20... | collective-permute-start | bytes 786440 | tf_op jit(solution)/shard_map/ppermute | solution.py:111
  53.2 12.5 %collective-permute-start.8 = (bf16[1024,128]{1,0:T(8,128)(2,1)S(1)}, bf16[1024,128]{1,0:T(8,128)(2,1)S(1)}, u32[]{:S(2)}, u32[]{:S(2)}) collective-permute-start(bf16[1024,128]{1,0:T(8,128)(2,1)S(1)} %add_convert_fusion.21), channel_id=1, source_target_pairs={{8,16},{16,8},{9,17},{17,9},{10,18},{18,10},{11,19},{19,11},{12,20... | collective-permute-start | bytes 786440 | tf_op jit(solution)/shard_map/ppermute | solution.py:111
  58.8 8.3 %collective-permute-start.35 = (bf16[1024,128]{1,0:T(8,128)(2,1)S(1)}, bf16[1024,128]{1,0:T(8,128)(2,1)S(1)}, u32[]{:S(2)}, u32[]{:S(2)}) collective-permute-start(bf16[1024,128]{1,0:T(8,128)(2,1)S(1)} %add_convert_fusion.11), channel_id=1, source_target_pairs={{8,16},{16,8},{9,17},{17,9},{10,18},{18,10},{11,19},{19,11},{12,20... | collective-permute-start | bytes 786440 | tf_op jit(solution)/shard_map/ppermute | solution.py:111
  63.7 4.9 %collective-permute-start.38 = (bf16[1024,128]{1,0:T(8,128)(2,1)S(1)}, bf16[1024,128]{1,0:T(8,128)(2,1)S(1)}, u32[]{:S(2)}, u32[]{:S(2)}) collective-permute-start(bf16[1024,128]{1,0:T(8,128)(2,1)S(1)} %add_convert_fusion.9), channel_id=1, source_target_pairs={{8,16},{16,8},{9,17},{17,9},{10,18},{18,10},{11,19},{19,11},{12,20... | collective-permute-start | bytes 786440 | tf_op jit(solution)/shard_map/ppermute | solution.py:111
  64.4 13.8 %collective-permute-start.6 = (bf16[1024,128]{1,0:T(8,128)(2,1)S(1)}, bf16[1024,128]{1,0:T(8,128)(2,1)S(1)}, u32[]{:S(2)}, u32[]{:S(2)}) collective-permute-start(bf16[1024,128]{1,0:T(8,128)(2,1)S(1)} %add_convert_fusion.22), channel_id=1, source_target_pairs={{8,0},{16,24},{9,1},{17,25},{10,2},{18,26},{11,3},{19,27},{12,4},{... | collective-permute-start | bytes 786440 | tf_op jit(solution)/shard_map/ppermute | solution.py:115
  65.8 18.0 %collective-permute-start.9 = (bf16[1024,128]{1,0:T(8,128)(2,1)S(1)}, bf16[1024,128]{1,0:T(8,128)(2,1)S(1)}, u32[]{:S(2)}, u32[]{:S(2)}) collective-permute-start(bf16[1024,128]{1,0:T(8,128)(2,1)S(1)} %add_convert_fusion.20), channel_id=1, source_target_pairs={{8,0},{16,24},{9,1},{17,25},{10,2},{18,26},{11,3},{19,27},{12,4},{... | collective-permute-start | bytes 786440 | tf_op jit(solution)/shard_map/ppermute | solution.py:115
  67.2 22.2 %collective-permute-start.36 = (bf16[1024,128]{1,0:T(8,128)(2,1)S(1)}, bf16[1024,128]{1,0:T(8,128)(2,1)S(1)}, u32[]{:S(2)}, u32[]{:S(2)}) collective-permute-start(bf16[1024,128]{1,0:T(8,128)(2,1)S(1)} %add_convert_fusion.10), channel_id=1, source_target_pairs={{8,0},{16,24},{9,1},{17,25},{10,2},{18,26},{11,3},{19,27},{12,4},{... | collective-permute-start | bytes 786440 | tf_op jit(solution)/shard_map/ppermute | solution.py:115
  68.6 24.8 %collective-permute-start.39 = (bf16[1024,128]{1,0:T(8,128)(2,1)S(1)}, bf16[1024,128]{1,0:T(8,128)(2,1)}, u32[]{:S(2)}, u32[]{:S(2)}) collective-permute-start(bf16[1024,128]{1,0:T(8,128)(2,1)S(1)} %add_convert_fusion.8), channel_id=1, source_target_pairs={{8,0},{16,24},{9,1},{17,25},{10,2},{18,26},{11,3},{19,27},{12,4},{... | collective-permute-start | bytes 786440 | tf_op jit(solution)/shard_map/ppermute | solution.py:115
  105.0 6.4 %collective-permute-start.11 = (bf16[1024,128]{1,0:T(8,128)(2,1)S(1)}, bf16[1024,128]{1,0:T(8,128)(2,1)S(1)}, u32[]{:S(2)}, u32[]{:S(2)}) collective-permute-start(bf16[1024,128]{1,0:T(8,128)(2,1)S(1)} %fusion.16), channel_id=1, source_target_pairs={{0,2},{1,5},{2,0},{3,7},{4,6},{5,1},{6,4},{7,3},{8,10},{9,13},{10,... | collective-permute-start | bytes 786440 | tf_op jit(solution)/shard_map/ppermute | solution.py:99
  106.7 8.3 %collective-permute-start.41 = (bf16[1024,128]{1,0:T(8,128)(2,1)S(1)}, bf16[1024,128]{1,0:T(8,128)(2,1)S(1)}, u32[]{:S(2)}, u32[]{:S(2)}) collective-permute-start(bf16[1024,128]{1,0:T(8,128)(2,1)S(1)} %fusion.19), channel_id=1, source_target_pairs={{0,2},{1,5},{2,0},{3,7},{4,6},{5,1},{6,4},{7,3},{8,10},{9,13},{10,... | collective-permute-start | bytes 786440 | tf_op jit(solution)/shard_map/ppermute | solution.py:99
  111.6 7.0 %collective-permute-start.12 = (bf16[1024,128]{1,0:T(8,128)(2,1)S(1)}, bf16[1024,128]{1,0:T(8,128)(2,1)S(1)}, u32[]{:S(2)}, u32[]{:S(2)}) collective-permute-start(bf16[1024,128]{1,0:T(8,128)(2,1)S(1)} %fusion.26), channel_id=1, source_target_pairs={{0,4},{1,3},{2,6},{3,1},{4,0},{5,7},{6,2},{7,5},{8,12},{9,11},{10,... | collective-permute-start | bytes 786440 | tf_op jit(solution)/shard_map/ppermute | solution.py:99
  115.1 6.4 %collective-permute-start.42 = (bf16[1024,128]{1,0:T(8,128)(2,1)S(1)}, bf16[1024,128]{1,0:T(8,128)(2,1)S(1)}, u32[]{:S(2)}, u32[]{:S(2)}) collective-permute-start(bf16[1024,128]{1,0:T(8,128)(2,1)S(1)} %fusion.29), channel_id=1, source_target_pairs={{0,4},{1,3},{2,6},{3,1},{4,0},{5,7},{6,2},{7,5},{8,12},{9,11},{10,... | collective-permute-start | bytes 786440 | tf_op jit(solution)/shard_map/ppermute | solution.py:99
  122.3 9.0 %collective-permute-start.43 = (bf16[1024,128]{1,0:T(8,128)(2,1)S(1)}, bf16[1024,128]{1,0:T(8,128)(2,1)S(1)}, u32[]{:S(2)}, u32[]{:S(2)}) collective-permute-start(bf16[1024,128]{1,0:T(8,128)(2,1)S(1)} %get-tuple-element.32.w_own), channel_id=1, source_target_pairs={{0,1},{1,0},{2,3},{3,2},{4,5},{5,4},{6,7},{7,6},{8,9},{9,8},{10,11... | collective-permute-start | bytes 786440 | tf_op jit(solution)/shard_map/ppermute | solution.py:145
  127.9 7.9 %collective-permute-start.14 = (bf16[1024,128]{1,0:T(8,128)(2,1)S(1)}, bf16[1024,128]{1,0:T(8,128)(2,1)S(1)}, u32[]{:S(2)}, u32[]{:S(2)}) collective-permute-start(bf16[1024,128]{1,0:T(8,128)(2,1)S(1)} %backward.14), channel_id=1, source_target_pairs={{0,8},{24,16},{1,9},{25,17},{2,10},{26,18},{3,11},{27,19},{4,12},{... | collective-permute-start | bytes 786440 | tf_op jit(solution)/shard_map/ppermute | solution.py:108
  130.0 11.4 %collective-permute-start.17 = (bf16[1024,128]{1,0:T(8,128)(2,1)S(1)}, bf16[1024,128]{1,0:T(8,128)(2,1)S(1)}, u32[]{:S(2)}, u32[]{:S(2)}) collective-permute-start(bf16[1024,128]{1,0:T(8,128)(2,1)S(1)} %backward.15), channel_id=1, source_target_pairs={{0,8},{24,16},{1,9},{25,17},{2,10},{26,18},{3,11},{27,19},{4,12},{... | collective-permute-start | bytes 786440 | tf_op jit(solution)/shard_map/ppermute | solution.py:108
  132.2 14.8 %collective-permute-start.44 = (bf16[1024,128]{1,0:T(8,128)(2,1)S(1)}, bf16[1024,128]{1,0:T(8,128)(2,1)S(1)}, u32[]{:S(2)}, u32[]{:S(2)}) collective-permute-start(bf16[1024,128]{1,0:T(8,128)(2,1)S(1)} %backward.20), channel_id=1, source_target_pairs={{0,8},{24,16},{1,9},{25,17},{2,10},{26,18},{3,11},{27,19},{4,12},{... | collective-permute-start | bytes 786440 | tf_op jit(solution)/shard_map/ppermute | solution.py:108
  134.3 17.8 %collective-permute-start.47 = (bf16[1024,128]{1,0:T(8,128)(2,1)S(1)}, bf16[1024,128]{1,0:T(8,128)(2,1)S(1)}, u32[]{:S(2)}, u32[]{:S(2)}) collective-permute-start(bf16[1024,128]{1,0:T(8,128)(2,1)S(1)} %backward.21), channel_id=1, source_target_pairs={{0,8},{24,16},{1,9},{25,17},{2,10},{26,18},{3,11},{27,19},{4,12},{... | collective-permute-start | bytes 786440 | tf_op jit(solution)/shard_map/ppermute | solution.py:108
  135.9 17.0 %collective-permute-start.15 = (bf16[1024,128]{1,0:T(8,128)(2,1)S(1)}, bf16[1024,128]{1,0:T(8,128)(2,1)S(1)}, u32[]{:S(2)}, u32[]{:S(2)}) collective-permute-start(bf16[1024,128]{1,0:T(8,128)(2,1)S(1)} %add_convert_fusion.19), channel_id=1, source_target_pairs={{8,16},{16,8},{9,17},{17,9},{10,18},{18,10},{11,19},{19,11},{12,20... | collective-permute-start | bytes 786440 | tf_op jit(solution)/shard_map/ppermute | solution.py:111
  141.5 12.8 %collective-permute-start.18 = (bf16[1024,128]{1,0:T(8,128)(2,1)S(1)}, bf16[1024,128]{1,0:T(8,128)(2,1)S(1)}, u32[]{:S(2)}, u32[]{:S(2)}) collective-permute-start(bf16[1024,128]{1,0:T(8,128)(2,1)S(1)} %add_convert_fusion.17), channel_id=1, source_target_pairs={{8,16},{16,8},{9,17},{17,9},{10,18},{18,10},{11,19},{19,11},{12,20... | collective-permute-start | bytes 786440 | tf_op jit(solution)/shard_map/ppermute | solution.py:111
  147.1 8.6 %collective-permute-start.45 = (bf16[1024,128]{1,0:T(8,128)(2,1)S(1)}, bf16[1024,128]{1,0:T(8,128)(2,1)S(1)}, u32[]{:S(2)}, u32[]{:S(2)}) collective-permute-start(bf16[1024,128]{1,0:T(8,128)(2,1)S(1)} %add_convert_fusion.7), channel_id=1, source_target_pairs={{8,16},{16,8},{9,17},{17,9},{10,18},{18,10},{11,19},{19,11},{12,20... | collective-permute-start | bytes 786440 | tf_op jit(solution)/shard_map/ppermute | solution.py:111
  152.2 5.0 %collective-permute-start.48 = (bf16[1024,128]{1,0:T(8,128)(2,1)S(1)}, bf16[1024,128]{1,0:T(8,128)(2,1)S(1)}, u32[]{:S(2)}, u32[]{:S(2)}) collective-permute-start(bf16[1024,128]{1,0:T(8,128)(2,1)S(1)} %add_convert_fusion.5), channel_id=1, source_target_pairs={{8,16},{16,8},{9,17},{17,9},{10,18},{18,10},{11,19},{19,11},{12,20... | collective-permute-start | bytes 786440 | tf_op jit(solution)/shard_map/ppermute | solution.py:111
  153.0 12.6 %collective-permute-start.16 = (bf16[1024,128]{1,0:T(8,128)(2,1)S(1)}, bf16[1024,128]{1,0:T(8,128)(2,1)S(1)}, u32[]{:S(2)}, u32[]{:S(2)}) collective-permute-start(bf16[1024,128]{1,0:T(8,128)(2,1)S(1)} %add_convert_fusion.18), channel_id=1, source_target_pairs={{8,0},{16,24},{9,1},{17,25},{10,2},{18,26},{11,3},{19,27},{12,4},{... | collective-permute-start | bytes 786440 | tf_op jit(solution)/shard_map/ppermute | solution.py:115
  154.4 16.9 %collective-permute-start.19 = (bf16[1024,128]{1,0:T(8,128)(2,1)S(1)}, bf16[1024,128]{1,0:T(8,128)(2,1)S(1)}, u32[]{:S(2)}, u32[]{:S(2)}) collective-permute-start(bf16[1024,128]{1,0:T(8,128)(2,1)S(1)} %add_convert_fusion.16), channel_id=1, source_target_pairs={{8,0},{16,24},{9,1},{17,25},{10,2},{18,26},{11,3},{19,27},{12,4},{... | collective-permute-start | bytes 786440 | tf_op jit(solution)/shard_map/ppermute | solution.py:115
  155.8 21.1 %collective-permute-start.46 = (bf16[1024,128]{1,0:T(8,128)(2,1)S(1)}, bf16[1024,128]{1,0:T(8,128)(2,1)S(1)}, u32[]{:S(2)}, u32[]{:S(2)}) collective-permute-start(bf16[1024,128]{1,0:T(8,128)(2,1)S(1)} %add_convert_fusion.6), channel_id=1, source_target_pairs={{8,0},{16,24},{9,1},{17,25},{10,2},{18,26},{11,3},{19,27},{12,4},{... | collective-permute-start | bytes 786440 | tf_op jit(solution)/shard_map/ppermute | solution.py:115
  157.3 23.8 %collective-permute-start.49 = (bf16[1024,128]{1,0:T(8,128)(2,1)S(1)}, bf16[1024,128]{1,0:T(8,128)(2,1)S(1)}, u32[]{:S(2)}, u32[]{:S(2)}) collective-permute-start(bf16[1024,128]{1,0:T(8,128)(2,1)S(1)} %add_convert_fusion.4), channel_id=1, source_target_pairs={{8,0},{16,24},{9,1},{17,25},{10,2},{18,26},{11,3},{19,27},{12,4},{... | collective-permute-start | bytes 786440 | tf_op jit(solution)/shard_map/ppermute | solution.py:115
  179.9 5.0 %collective-permute-start.20 = (bf16[1024,128]{1,0:T(8,128)(2,1)S(1)}, bf16[1024,128]{1,0:T(8,128)(2,1)S(1)}, u32[]{:S(2)}, u32[]{:S(2)}) collective-permute-start(bf16[1024,128]{1,0:T(8,128)(2,1)S(1)} %get-tuple-element.19), channel_id=1, source_target_pairs={{0,1},{1,0},{2,3},{3,2},{4,5},{5,4},{6,7},{7,6},{8,9},{9,8},{10,11... | collective-permute-start | bytes 786440 | tf_op jit(solution)/shard_map/ppermute | solution.py:95
  185.0 6.4 %collective-permute-start.21 = (bf16[1024,128]{1,0:T(8,128)(2,1)S(1)}, bf16[1024,128]{1,0:T(8,128)(2,1)S(1)}, u32[]{:S(2)}, u32[]{:S(2)}) collective-permute-start(bf16[1024,128]{1,0:T(8,128)(2,1)S(1)} %fusion.17), channel_id=1, source_target_pairs={{0,2},{1,5},{2,0},{3,7},{4,6},{5,1},{6,4},{7,3},{8,10},{9,13},{10,... | collective-permute-start | bytes 786440 | tf_op jit(solution)/shard_map/ppermute | solution.py:99
  186.6 7.9 %collective-permute-start.51 = (bf16[1024,128]{1,0:T(8,128)(2,1)S(1)}, bf16[1024,128]{1,0:T(8,128)(2,1)S(1)}, u32[]{:S(2)}, u32[]{:S(2)}) collective-permute-start(bf16[1024,128]{1,0:T(8,128)(2,1)S(1)} %fusion.20), channel_id=1, source_target_pairs={{0,2},{1,5},{2,0},{3,7},{4,6},{5,1},{6,4},{7,3},{8,10},{9,13},{10,... | collective-permute-start | bytes 786440 | tf_op jit(solution)/shard_map/ppermute | solution.py:99
  191.5 6.4 %collective-permute-start.22 = (bf16[1024,128]{1,0:T(8,128)(2,1)S(1)}, bf16[1024,128]{1,0:T(8,128)(2,1)S(1)}, u32[]{:S(2)}, u32[]{:S(2)}) collective-permute-start(bf16[1024,128]{1,0:T(8,128)(2,1)S(1)} %fusion.27), channel_id=1, source_target_pairs={{0,4},{1,3},{2,6},{3,1},{4,0},{5,7},{6,2},{7,5},{8,12},{9,11},{10,... | collective-permute-start | bytes 786440 | tf_op jit(solution)/shard_map/ppermute | solution.py:99
  194.7 6.4 %collective-permute-start.52 = (bf16[1024,128]{1,0:T(8,128)(2,1)S(1)}, bf16[1024,128]{1,0:T(8,128)(2,1)S(1)}, u32[]{:S(2)}, u32[]{:S(2)}) collective-permute-start(bf16[1024,128]{1,0:T(8,128)(2,1)S(1)} %fusion.30), channel_id=1, source_target_pairs={{0,4},{1,3},{2,6},{3,1},{4,0},{5,7},{6,2},{7,5},{8,12},{9,11},{10,... | collective-permute-start | bytes 786440 | tf_op jit(solution)/shard_map/ppermute | solution.py:99
  203.0 5.7 %collective-permute-start.53 = (bf16[1024,128]{1,0:T(8,128)(2,1)S(1)}, bf16[1024,128]{1,0:T(8,128)(2,1)S(1)}, u32[]{:S(2)}, u32[]{:S(2)}) collective-permute-start(bf16[1024,128]{1,0:T(8,128)(2,1)S(1)} %get-tuple-element.30.w_own), channel_id=1, source_target_pairs={{0,1},{1,0},{2,3},{3,2},{4,5},{5,4},{6,7},{7,6},{8,9},{9,8},{10,11... | collective-permute-start | bytes 786440 | tf_op jit(solution)/shard_map/ppermute | solution.py:145
  205.2 24.7 %collective-permute-start.24 = (bf16[1024,128]{1,0:T(8,128)(2,1)S(1)}, bf16[1024,128]{1,0:T(8,128)(2,1)S(1)}, u32[]{:S(2)}, u32[]{:S(2)}) collective-permute-start(bf16[1024,128]{1,0:T(8,128)(2,1)S(1)} %backward.16), channel_id=1, source_target_pairs={{0,8},{24,16},{1,9},{25,17},{2,10},{26,18},{3,11},{27,19},{4,12},{... | collective-permute-start | bytes 786440 | tf_op jit(solution)/shard_map/ppermute | solution.py:108
  207.4 23.3 %collective-permute-start.27 = (bf16[1024,128]{1,0:T(8,128)(2,1)S(1)}, bf16[1024,128]{1,0:T(8,128)(2,1)S(1)}, u32[]{:S(2)}, u32[]{:S(2)}) collective-permute-start(bf16[1024,128]{1,0:T(8,128)(2,1)S(1)} %backward.17), channel_id=1, source_target_pairs={{0,8},{24,16},{1,9},{25,17},{2,10},{26,18},{3,11},{27,19},{4,12},{... | collective-permute-start | bytes 786440 | tf_op jit(solution)/shard_map/ppermute | solution.py:108
  209.5 22.0 %collective-permute-start.54 = (bf16[1024,128]{1,0:T(8,128)(2,1)S(1)}, bf16[1024,128]{1,0:T(8,128)(2,1)S(1)}, u32[]{:S(2)}, u32[]{:S(2)}) collective-permute-start(bf16[1024,128]{1,0:T(8,128)(2,1)S(1)} %backward.22), channel_id=1, source_target_pairs={{0,8},{24,16},{1,9},{25,17},{2,10},{26,18},{3,11},{27,19},{4,12},{... | collective-permute-start | bytes 786440 | tf_op jit(solution)/shard_map/ppermute | solution.py:108
  211.7 20.6 %collective-permute-start.57 = (bf16[1024,128]{1,0:T(8,128)(2,1)S(1)}, bf16[1024,128]{1,0:T(8,128)(2,1)S(1)}, u32[]{:S(2)}, u32[]{:S(2)}) collective-permute-start(bf16[1024,128]{1,0:T(8,128)(2,1)S(1)} %backward.23), channel_id=1, source_target_pairs={{0,8},{24,16},{1,9},{25,17},{2,10},{26,18},{3,11},{27,19},{4,12},{... | collective-permute-start | bytes 786440 | tf_op jit(solution)/shard_map/ppermute | solution.py:108
  233.1 15.7 %collective-permute-start.26 = (bf16[1024,128]{1,0:T(8,128)(2,1)S(1)}, bf16[1024,128]{1,0:T(8,128)(2,1)S(1)}, u32[]{:S(2)}, u32[]{:S(2)}) collective-permute-start(bf16[1024,128]{1,0:T(8,128)(2,1)S(1)} %add_convert_fusion.14), channel_id=1, source_target_pairs={{8,0},{16,24},{9,1},{17,25},{10,2},{18,26},{11,3},{19,27},{12,4},{... | collective-permute-start | bytes 786440 | tf_op jit(solution)/shard_map/ppermute | solution.py:115
  234.5 19.9 %collective-permute-start.29 = (bf16[1024,128]{1,0:T(8,128)(2,1)S(1)}, bf16[1024,128]{1,0:T(8,128)(2,1)S(1)}, u32[]{:S(2)}, u32[]{:S(2)}) collective-permute-start(bf16[1024,128]{1,0:T(8,128)(2,1)S(1)} %add_convert_fusion.12), channel_id=1, source_target_pairs={{8,0},{16,24},{9,1},{17,25},{10,2},{18,26},{11,3},{19,27},{12,4},{... | collective-permute-start | bytes 786440 | tf_op jit(solution)/shard_map/ppermute | solution.py:115
  235.9 24.2 %collective-permute-start.56 = (bf16[1024,128]{1,0:T(8,128)(2,1)S(1)}, bf16[1024,128]{1,0:T(8,128)(2,1)S(1)}, u32[]{:S(2)}, u32[]{:S(2)}) collective-permute-start(bf16[1024,128]{1,0:T(8,128)(2,1)S(1)} %add_convert_fusion.2), channel_id=1, source_target_pairs={{8,0},{16,24},{9,1},{17,25},{10,2},{18,26},{11,3},{19,27},{12,4},{... | collective-permute-start | bytes 786440 | tf_op jit(solution)/shard_map/ppermute | solution.py:115
  237.3 27.0 %collective-permute-start.59 = (bf16[1024,128]{1,0:T(8,128)(2,1)S(1)}, bf16[1024,128]{1,0:T(8,128)(2,1)S(1)}, u32[]{:S(2)}, u32[]{:S(2)}) collective-permute-start(bf16[1024,128]{1,0:T(8,128)(2,1)S(1)} %add_convert_fusion), channel_id=1, source_target_pairs={{8,0},{16,24},{9,1},{17,25},{10,2},{18,26},{11,3},{19,27},{12,4},{... | collective-permute-start | bytes 786440 | tf_op jit(solution)/shard_map/ppermute | solution.py:115
  (55 other events, 466.2 us)

commit v2 on v0

v2 whole, which is shorter than its diff:
```python
import functools

import jax
import jax.numpy as jnp
from jax import lax
from jax.experimental import pallas as pl
from jax.experimental.pallas import tpu as pltpu
from jax.sharding import PartitionSpec as P

RATE = 2.0
PARTS = 4
F32 = jnp.float32
BF16 = jnp.bfloat16
ANY = pl.BlockSpec(memory_space=pl.ANY)
VMEM = pl.BlockSpec(memory_space=pltpu.VMEM)
SMEM = pl.BlockSpec(memory_space=pltpu.SMEM)
FREE = pl.CostEstimate(flops=0, bytes_accessed=0, transcendentals=0)


def span(bit, size):
    return pl.ds(pl.multiple_of(bit * size, size), size)


def near(value):
    return pltpu.with_memory_space_constraint(value, pltpu.VMEM)


def call(body, outs, *operands, name, scratch=(), limit=12):
    return pl.pallas_call(
        body,
        in_specs=[SMEM] + [VMEM] * (len(operands) - 1),
        out_specs=[VMEM] * len(outs),
        out_shape=[pltpu.VMEM(shape, dtype) for shape, dtype in outs],
        scratch_shapes=[pltpu.VMEM(shape, dtype) for shape, dtype in scratch],
        compiler_params=pltpu.CompilerParams(vmem_limit_bytes=limit << 20),
        cost_estimate=FREE,
        name=name,
    )(operands[0], *[near(v) for v in operands[1:]])


def hold_kernel(source, *refs):
    out, sem = refs[-2:]
    copy = pltpu.make_async_copy(source, out, sem)
    copy.start()
    copy.wait()


def hold(z, *others):
    return pl.pallas_call(
        hold_kernel,
        in_specs=[pl.BlockSpec(memory_space=pltpu.HBM)] + [ANY for _ in others],
        out_specs=VMEM,
        out_shape=pltpu.VMEM(z.shape, z.dtype),
        scratch_shapes=[pltpu.SemaphoreType.DMA],
        compiler_params=pltpu.CompilerParams(vmem_limit_bytes=10 << 20),
        cost_estimate=FREE,
        name="hold",
    )(pltpu.with_memory_space_constraint(z, pltpu.HBM), *others)


def prepare_kernel(halves, index, logits, labels, residual, *curvatures):
    probability = jax.nn.sigmoid(logits[0])
    residual[...] = (probability - labels[...].astype(F32)).astype(BF16)

    @pl.when(pl.program_id(0) < halves)
    def _():
        cols = curvatures[0].shape[1]
        for c, curvature in enumerate(curvatures):
            mine = probability[:, c * cols : (c + 1) * cols]
            curvature[...] = mine * (1.0 - mine)


def prepare(index, logits, labels, step):
    _, rows, depth = logits.shape
    block = min(256, rows // 2)
    count = rows // block
    place = lambda i, index: ((i + index[0] * (count // 2)) % count, 0)
    own = pl.BlockSpec((block, depth // 2), lambda i, index: (jnp.minimum(i, count // 2 - 1), 0))
    return pl.pallas_call(
        functools.partial(prepare_kernel, count // 2),
        grid_spec=pltpu.PrefetchScalarGridSpec(
            num_scalar_prefetch=1,
            grid=(count,),
            in_specs=[
                pl.BlockSpec((1, block, depth), lambda i, index: (step, *place(i, index))),
                pl.BlockSpec((block, depth), place),
            ],
            out_specs=[pl.BlockSpec((block, depth), place), own, own],
        ),
        out_shape=[jax.ShapeDtypeStruct((rows, depth), BF16)]
        + [jax.ShapeDtypeStruct((rows // 2, depth // 2), F32)] * 2,
        compiler_params=pltpu.CompilerParams(vmem_limit_bytes=12 << 20),
        cost_estimate=FREE,
        name="prepare",
    )(index, logits, labels)


def part_out(index, which, total, kept, sent):
    half = kept.shape[0]
    sent[...] = total[span(1 - index[which], half), :].astype(BF16)
    kept[...] = total[span(index[which], half), :]


def first_kernel(start, out):
    out[...] = start[...]


def columns(start, c):
    count, depth = start.shape
    return pl.pallas_call(
        first_kernel,
        grid=(1,),
        in_specs=[pl.BlockSpec((count, depth // 2), lambda i: (0, c))],
        out_specs=pl.BlockSpec((count, depth // 2), lambda i: (0, 0)),
        out_shape=jax.ShapeDtypeStruct((count, depth // 2), F32),
        compiler_params=pltpu.CompilerParams(vmem_limit_bytes=12 << 20),
        cost_estimate=FREE,
        name="columns",
    )(start)


def forward_kernel(updates, index, z, adjoint, *refs):
    hessian, (*new, low, kept, sent, total) = refs[:updates], refs[updates:]
    if updates:
        half = hessian[0].shape[0]
        for bit, h in zip((index[1], 1 - index[1]), hessian):
            rows = span(bit, half)
            value = adjoint[rows, :] - RATE * h[...].astype(F32)
            new[0][rows, :] = value
            low[rows, :] = value.astype(BF16)
    else:
        low[...] = adjoint[...].astype(BF16)
    total[...] = jnp.dot(z[...], low[...], preferred_element_type=F32)
    part_out(index, 0, total, kept, sent)


def forward(index, z, adjoint, hessian):
    (rows, width), cols = z.shape, adjoint.shape[1]
    outs = [((width, cols), F32)] if hessian else []
    outs += [((width, cols), BF16), ((rows // 2, cols), F32), ((rows // 2, cols), BF16)]
    body = functools.partial(forward_kernel, len(hessian))
    out = call(body, outs, index, z, adjoint, *hessian, name="forward", scratch=[((rows, cols), F32)])
    return out if hessian else [adjoint, *out]


def add_kernel(index, one, two, total, low):
    value = one[...] + two[...].astype(F32)
    total[...] = value
    low[...] = value.astype(BF16)


def add(index, one, two):
    return call(add_kernel, [(one.shape, F32), (one.shape, BF16)], index, one, two, name="add")


def weigh_kernel(index, one, two, curvature, out):
    out[...] = (curvature[...] * (one[...] + two[...].astype(F32))).astype(BF16)


def weigh(index, one, two, curvature):
    return call(weigh_kernel, [(one.shape, BF16)], index, one, two, curvature, name="weigh")[0]


def backward_kernel(index, z, w_own, w_other, weight, kept, sent, total):
    half = w_own.shape[0]
    weight[span(index[0], half), :] = w_own[...]
    weight[span(1 - index[0], half), :] = w_other[...]
    dims = (((0,), (0,)), ((), ()))
    total[...] = lax.dot_general(weight[...], z[...], dims, preferred_element_type=F32).T
    part_out(index, 1, total, kept, sent)


def backward(index, z, w_own, w_other):
    (rows, width), cols = z.shape, w_own.shape[1]
    outs = [((rows, cols), BF16), ((width // 2, cols), F32), ((width // 2, cols), BF16)]
    return call(
        backward_kernel, outs, index, z, w_own, w_other, name="backward", scratch=[((width, cols), F32)]
    )


def merge_kernel(index, one, two, out):
    out[...] = (one[...].astype(F32) + two[...].astype(F32)).astype(BF16)


def merge(index, one, two):
    return call(merge_kernel, [(one.shape, BF16)], index, one, two, name="merge")[0]


def join_kernel(index, one, two, out):
    cols = one.shape[1]
    out[:, :cols] = one[...]
    out[:, cols:] = two[...]


def join(index, one, two):
    return call(join_kernel, [((one.shape[0], 2 * one.shape[1]), BF16)], index, one, two, name="join")[0]


def finish_kernel(index, adjoint, own, other, *refs):
    out, half = refs[-1], own.shape[0]
    for bit, h in zip((index[1], 1 - index[1]), (own, other)):
        rows = span(bit, half)
        out[rows, :] = adjoint[rows, :] - RATE * h[...].astype(F32)


def finish(index, adjoint, hessian, c, held):
    count, cols = adjoint.shape
    return pl.pallas_call(
        finish_kernel,
        grid=(1,),
        in_specs=[SMEM, VMEM, VMEM, VMEM] + [ANY for _ in held],
        out_specs=pl.BlockSpec((count, cols), lambda i: (0, c)),
        out_shape=jax.ShapeDtypeStruct((count, 2 * cols), F32),
        input_output_aliases={4: 0} if held else {},
        compiler_params=pltpu.CompilerParams(vmem_limit_bytes=12 << 20),
        cost_estimate=FREE,
        name="finish",
    )(index, *[near(v) for v in (adjoint, *hessian)], *held)


def outer_kernel(steps, *refs):
    residuals, weights, lows = refs[:steps], refs[steps : 2 * steps], refs[2 * steps : 3 * steps]
    coefficients, out = refs[3 * steps], refs[-1]
    dims = (((1,), (1,)), ((), ()))
    pairs = [(r[...], b[...]) for r, b in zip(residuals, lows)]
    pairs += [(w[...], coefficients[steps - 1 - k]) for k, w in enumerate(weights)]
    total = lax.dot_general(*pairs[0], dims, preferred_element_type=F32)
    for a, b in pairs[1:]:
        total += lax.dot_general(a, b, dims, preferred_element_type=F32)
    out[...] = -RATE * total


def outer(residuals, weights, lows, coefficients, part, held):
    rows, depth = residuals[0].shape
    steps, cols = coefficients.shape[:2]
    block = min(256, rows // PARTS)
    count = rows // PARTS // block
    first = part * count
    left = [*residuals, *weights]
    return pl.pallas_call(
        functools.partial(outer_kernel, steps),
        grid=(count,),
        in_specs=[pl.BlockSpec((block, depth), lambda i: (first + i, 0)) for _ in left]
        + [VMEM] * (steps + 1)
        + [ANY for _ in held],
        out_specs=pl.BlockSpec((block, cols), lambda i: (first + i, 0)),
        out_shape=jax.ShapeDtypeStruct((rows, cols), F32),
        input_output_aliases={3 * steps + 1: 0} if held else {},
        compiler_params=pltpu.CompilerParams(vmem_limit_bytes=14 << 20),
        cost_estimate=FREE,
        name="outer",
    )(*left, *[near(v) for v in (*lows, coefficients)], *held)


def swap(value, axis, count, bit):
    return lax.ppermute(value, axis, [(i, i ^ bit) for i in range(count)])


class Turn:
    def __init__(self):
        self.last = ()

    def begin(self, *values):
        return lax.optimization_barrier((*values, *self.last))[: len(values)]

    def end(self, value):
        self.last = (value,)


def chain(turn, counts, index, z, curvature, adjoint, steps):
    rows_count, inst_count = counts
    crossings = [1 << b for b in range(1, inst_count.bit_length() - 1)]
    crossings_row = [1 << b for b in range(1, rows_count.bit_length() - 1)]
    hessian = ()
    for step in range(steps - 1, -1, -1):
        adjoint, *hessian = turn.begin(adjoint, *hessian)
        adjoint, low, product, sent = forward(index, z, adjoint, hessian)
        turn.end(product)
        sent = swap(sent, "inst", inst_count, 1)
        yield "V", low
        for k in range(len(crossings)):
            product, sent = turn.begin(product, sent)
            product, moved = add(index, product, sent)
            turn.end(moved)
            bits = (crossings[k], crossings[(k + 1) % len(crossings)])
            sent = lax.ppermute(moved, "inst", [(i, i ^ bits[i & 1]) for i in range(inst_count)])
            yield f"x{k}", None
        product, sent = turn.begin(product, sent)
        w_own = weigh(index, product, sent, curvature[step])
        turn.end(w_own)
        w_other = swap(w_own, "inst", inst_count, 1)
        yield "W", None
        w_own, w_other = turn.begin(w_own, w_other)
        weight, total, sent = backward(index, z, w_own, w_other)
        turn.end(total)
        if rows_count > 1:
            sent = swap(sent, "row", rows_count, 1)
        yield "H", weight
        if rows_count > 1:
            for k in range(len(crossings_row) + 1):
                total, sent = turn.begin(total, sent)
                total = merge(index, total, sent)
                turn.end(total)
                sent = swap(total, "row", rows_count, (crossings_row + [1])[k])
                yield f"z{k}", None
        hessian = (total, sent)
    yield "end", adjoint, hessian


def shards(rows_count, inst_count, design, labels, saved_logits, saved_coefficients, cotangent):
    steps = saved_logits.shape[0]
    core = lax.axis_index("inst") % 2
    side = lax.axis_index("row") % 2
    index = jnp.stack([core, side]).astype(jnp.int32)
    starts = [columns(cotangent, c) for c in range(2)]
    z = hold(design, index)
    turn = Turn()
    prepared = [prepare(index, saved_logits, labels, step) for step in range(steps)]
    residuals = [p[0] for p in prepared[::-1]]
    chains = [
        chain(turn, (rows_count, inst_count), index, z, [p[1 + c] for p in prepared], starts[c], steps)
        for c in range(2)
    ]
    lows, weights = [], []

    def joined(value):
        (one,) = turn.begin(value[0])
        out = join(index, one, value[1])
        turn.end(out)
        return out

    parts, grad, first = 0, (), ()
    crossings = max(rows_count.bit_length() - 1, 0)
    for c in lagged(steps * (3 + max(inst_count.bit_length() - 2, 0) + crossings), LAG):
        stage, *values = next(chains[c])
        if stage == "V" and c:
            lows.append((seen, values[0]))
        elif stage == "V":
            seen = values[0]
        elif stage == "H" and c:
            weights.append((held, values[0]))
            lows[-1], weights[-1] = joined(lows[-1]), joined(weights[-1])
        elif stage == "H":
            held = values[0]
        if len(weights) == steps and parts < PARTS:
            grad = part_of(turn, residuals, weights, lows, saved_coefficients, parts, grad)
            parts += 1
    for c in range(2):
        _, adjoint, hessian = next(chains[c])
        if c == 1:
            while parts < PARTS:
                grad = part_of(turn, residuals, weights, lows, saved_coefficients, parts, grad)
                parts += 1
        adjoint, *hessian = turn.begin(adjoint, *hessian)
        first = (finish(index, adjoint, hessian, c, first),)
        turn.end(first[0])
    return first[0], grad[0]


def part_of(turn, residuals, weights, lows, coefficients, part, grad):
    low, *rest = turn.begin(lows[0], *lows[1:])
    grad = (outer(residuals, weights, [low, *rest], coefficients, part, grad),)
    turn.end(grad[0])
    return grad


LAG = 1


def lagged(total, lag):
    order = []
    for k in range(total + lag):
        order += [0] if k < total else []
        order += [1] if k >= lag else []
    return order


def plain(design, labels, saved_logits, saved_coefficients, cotangent):
    adjoint = cotangent
    accum = jnp.zeros(design.shape, F32)
    targets = labels.astype(F32)
    for step in range(saved_logits.shape[0] - 1, -1, -1):
        low = adjoint.astype(BF16)
        product = lax.psum(jnp.dot(design, low, preferred_element_type=F32), "inst")
        probability = jax.nn.sigmoid(saved_logits[step])
        residual = (probability - targets).astype(BF16)
        weighted = (probability * (1.0 - probability) * product).astype(BF16)
        accum = accum + jnp.dot(residual, low.T, preferred_element_type=F32)
        accum = accum + jnp.dot(weighted, saved_coefficients[step].T, preferred_element_type=F32)
        dims = (((0,), (0,)), ((), ()))
        hessian = lax.dot_general(design, weighted, dims, preferred_element_type=F32)
        adjoint = adjoint - RATE * lax.psum(hessian, "row")
    return adjoint, -RATE * accum


def solution(mesh):
    placed = (
        P("row", "inst"),
        P("row", None),
        P(None, "row", None),
        P(None, "inst", None),
        P("inst", None),
    )
    counts = (mesh.shape["row"], mesh.shape["inst"])
    even = counts[1] > 1 and all(n & (n - 1) == 0 for n in counts)
    return jax.shard_map(
        functools.partial(shards, *counts) if even else plain,
        mesh=mesh,
        in_specs=placed,
        out_specs=(P("inst", None), P("row", "inst")),
        check_vma=False,
    )
```

time: 524 us -> 218 us (0.42)
  waiting for transfers between devices: 355 us -> 85 us
  matrix products: 126 us -> 0 us
  Pallas kernels: 0 us -> 85.1 us
  starting transfers between devices: 0.65 us -> 43.6 us
  other arithmetic: 17.3 us -> 0.08 us
  between operations: 14.2 us -> 1.3 us
  local copies, waits for them, and re-layouts: 10.4 us -> 1.62 us
    psum x6 -> x0, waiting for transfers between devices: 355 us -> none  [the longest x3 190 us: shards(): hessian_term = lax.psum(local_hess, 'row')]
    dot_general x12 -> x0, matrix products: 126 us -> none  [the longest x3 53 us: shards(): jnp.dot(weighted, saved_coefficients[step].T, preferred_element_type=jnp....]
    pallas_call x0 -> x60, Pallas kernels: none -> 85.1 us  [the longest x48 54 us: call(): pl.pallas_call(body, in_specs=[SMEM] + [VMEM] * (len(operands) - 1), out_...]
    ppermute x0 -> x42, waiting for transfers between devices: none -> 85 us  [the longest x30 69.3 us: swap(): return lax.ppermute(value, axis, [(i, i ^ bit) for i in range(count)])]
    ppermute x0 -> x42, starting transfers between devices: none -> 43.6 us  [the longest x12 22.1 us: chain(): lax.ppermute(moved, 'inst', [(i, i ^ bits[i & 1]) for i in range(inst_cou...]
    convert_element_type x4 -> x0, other arithmetic: 10.5 us -> none  [the longest x3 8.55 us: shards(): weighted = (curvature * product).astype(jnp.bfloat16)]
    unnamed x20 -> x12, local copies, waits for them, and re-layouts: 10.4 us -> 1.62 us
    sub x2 -> x0, other arithmetic: 6.85 us -> none  [shards(): adjoint = adjoint - step_rate * hessian_term]
  transfers between devices with their start and end apart: 6 -> 42, of which waited for: 6 -> 26; matrix products, arithmetic and copies ran while one was open for 16% -> 0% of each run, Pallas kernels for 0% -> 35%
where the time goes in v2:
time: 218 us; the launch traced here: 217 us
  Pallas kernels  85.1 us (39%)
  waiting for transfers between devices  85 us (39%)
  starting transfers between devices  43.6 us (20%)
    ppermute x30, waiting for transfers between devices, swap(): return lax.ppermute(value, axis, [(i, i ^ bit) for i in range(count)])  69.3 us
    pallas_call x48, Pallas kernels, call(): pl.pallas_call(body, in_specs=[SMEM] + [VMEM] * (len(operands) - 1), out_...  54 us
    ppermute x12, starting transfers between devices, chain(): lax.ppermute(moved, 'inst', [(i, i ^ bits[i & 1]) for i in range(inst_cou...  22.1 us
    ppermute x30, starting transfers between devices, swap(): return lax.ppermute(value, axis, [(i, i ^ bit) for i in range(count)])  21.4 us
    pallas_call x4, Pallas kernels, outer(): pl.pallas_call(functools.partial(outer_kernel, steps), grid=(count,), in_...  20 us
    ppermute x12, waiting for transfers between devices, chain(): lax.ppermute(moved, 'inst', [(i, i ^ bits[i & 1]) for i in range(inst_cou...  15.6 us
    pallas_call x3, Pallas kernels, prepare(): pl.pallas_call(functools.partial(prepare_kernel, count // 2), grid_spec=p...  4.4 us
  transfers between devices with their start and end apart: 42, of which 26 were waited for; matrix products, arithmetic and copies ran while one was open for 0% of the time, Pallas kernels for 35%

profile of v2, /device:TPU:0, one launch (start us, length us, event | category | flops | bytes accessed | tf_op | source)
XLA Modules:
  0.0 216.6 jit_solution(9047309694733354077)
XLA Ops:
  2.4 3.4 %hold.1.z = bf16[2048,2048]{1,0:T(8,128)(2,1)S(1)} custom-call(bf16[2048,2048]{1,0:T(8,128)(2,1)} %source.1, s32[2]{0:T(128)S(1)} %pad_add_fusion.refs_0_.index), custom_call_target="tpu_custom_call" | custom-call | tf_op jit(solution)/shard_map/hold/pallas_call | solution.py:49
  5.8 3.1 %forward.6 = (bf16[2048,128]{1,0:T(8,128)(2,1)S(1)}, f32[1024,128]{1,0:T(8,128)S(1)}, bf16[1024,128]{1,0:T(8,128)(2,1)S(1)}) custom-call(s32[2]{0:T(128)S(1)} %pad_add_fusion.refs_0_.index, bf16[2048,2048]{1,0:T(8,128)(2,1)S(1)} %hold.1.z, f32[2048,128]{1,0:T(8,128)S(1)} %columns.3.adjoint), custom_call_target="tpu_custom_call" | custom-call | tf_op jit(solution)/shard_map/forward/pallas_call | solution.py:29
  11.2 2.9 %collective-permute-start.2 = (bf16[1024,128]{1,0:T(8,128)(2,1)S(1)}, bf16[1024,128]{1,0:T(8,128)(2,1)S(1)}, u32[]{:S(2)}, u32[]{:S(2)}) collective-permute-start(bf16[1024,128]{1,0:T(8,128)(2,1)S(1)} %get-tuple-element.188), channel_id=1, source_target_pairs={{0,2},{1,5},{2,0},{3,7},{4,6},{5,1},{6,4},{7,3},{8,10},{9,13},{10,... | collective-permute-start | bytes 786440 | tf_op jit(solution)/shard_map/ppermute | solution.py:286
  14.2 3.1 %forward.7 = (bf16[2048,128]{1,0:T(8,128)(2,1)S(1)}, f32[1024,128]{1,0:T(8,128)S(1)}, bf16[1024,128]{1,0:T(8,128)(2,1)S(1)}) custom-call(s32[2]{0:T(128)S(1)} %pad_add_fusion.refs_0_.index, bf16[2048,2048]{1,0:T(8,128)(2,1)S(1)} %hold.1.z, f32[2048,128]{1,0:T(8,128)S(1)} %columns.2.adjoint), custom_call_target="tpu_custom_call" | custom-call | tf_op jit(solution)/shard_map/forward/pallas_call | solution.py:29
  19.1 2.1 collective-permute-start.4
  24.9 2.9 %collective-permute-done.4.two = bf16[1024,128]{1,0:T(8,128)(2,1)S(1)} collective-permute-done((bf16[1024,128]{1,0:T(8,128)(2,1)S(1)}, bf16[1024,128]{1,0:T(8,128)(2,1)S(1)}, u32[]{:S(2)}, u32[]{:S(2)}) %collective-permute-start.4) | collective-permute-done | bytes 262176 | tf_op jit(solution)/shard_map/ppermute | solution.py:286
  29.1 2.5 %collective-permute-start.5 = (bf16[1024,128]{1,0:T(8,128)(2,1)S(1)}, bf16[1024,128]{1,0:T(8,128)(2,1)S(1)}, u32[]{:S(2)}, u32[]{:S(2)}) collective-permute-start(bf16[1024,128]{1,0:T(8,128)(2,1)S(1)} %get-tuple-element.207), channel_id=1, source_target_pairs={{0,4},{1,3},{2,6},{3,1},{4,0},{5,7},{6,2},{7,5},{8,12},{9,11},{10,... | collective-permute-start | bytes 786440 | tf_op jit(solution)/shard_map/ppermute | solution.py:286
  31.6 2.1 backward.6
  33.7 1.6 collective-permute-start.8
  36.7 4.8 %collective-permute-done.8.two = bf16[1024,128]{1,0:T(8,128)(2,1)S(1)} collective-permute-done((bf16[1024,128]{1,0:T(8,128)(2,1)S(1)}, bf16[1024,128]{1,0:T(8,128)(2,1)S(1)}, u32[]{:S(2)}, u32[]{:S(2)}) %collective-permute-start.8) | collective-permute-done | bytes 262176 | tf_op jit(solution)/shard_map/ppermute | solution.py:256
  42.1 2.8 %collective-permute-start.10 = (bf16[1024,128]{1,0:T(8,128)(2,1)S(1)}, bf16[1024,128]{1,0:T(8,128)(2,1)S(1)}, u32[]{:S(2)}, u32[]{:S(2)}) collective-permute-start(bf16[1024,128]{1,0:T(8,128)(2,1)S(1)} %merge.12.one), channel_id=1, source_target_pairs={{0,16},{8,24},{16,0},{24,8},{1,17},{9,25},{17,1},{25,9},{2,18},{10... | collective-permute-start | bytes 786440 | tf_op jit(solution)/shard_map/ppermute | solution.py:256
  44.9 2.1 backward.7
  47.0 1.6 collective-permute-start.9
  50.1 5.8 %collective-permute-done.10.two = bf16[1024,128]{1,0:T(8,128)(2,1)S(1)} collective-permute-done((bf16[1024,128]{1,0:T(8,128)(2,1)S(1)}, bf16[1024,128]{1,0:T(8,128)(2,1)S(1)}, u32[]{:S(2)}, u32[]{:S(2)}) %collective-permute-start.10) | collective-permute-done | bytes 262176 | tf_op jit(solution)/shard_map/ppermute | solution.py:256
  58.8 2.5 %collective-permute-start.11 = (bf16[1024,128]{1,0:T(8,128)(2,1)S(1)}, bf16[1024,128]{1,0:T(8,128)(2,1)S(1)}, u32[]{:S(2)}, u32[]{:S(2)}) collective-permute-start(bf16[1024,128]{1,0:T(8,128)(2,1)S(1)} %merge.14.one), channel_id=1, source_target_pairs={{0,16},{8,24},{16,0},{24,8},{1,17},{9,25},{17,1},{25,9},{2,18},{10... | collective-permute-start | bytes 786440 | tf_op jit(solution)/shard_map/ppermute | solution.py:256
  61.3 7.2 %collective-permute-done.12.refs_1_ = bf16[1024,128]{1,0:T(8,128)(2,1)S(1)} collective-permute-done((bf16[1024,128]{1,0:T(8,128)(2,1)S(1)}, bf16[1024,128]{1,0:T(8,128)(2,1)S(1)}, u32[]{:S(2)}, u32[]{:S(2)}) %collective-permute-start.12) | collective-permute-done | bytes 262176 | tf_op jit(solution)/shard_map/ppermute | solution.py:256
  68.5 3.2 %forward.8 = (f32[2048,128]{1,0:T(8,128)S(1)}, bf16[2048,128]{1,0:T(8,128)(2,1)S(1)}, f32[1024,128]{1,0:T(8,128)S(1)}, bf16[1024,128]{1,0:T(8,128)(2,1)S(1)}) custom-call(s32[2]{0:T(128)S(1)} %pad_add_fusion.refs_0_.index, bf16[2048,2048]{1,0:T(8,128)(2,1)S(1)} %hold.1.z, f32[2048,128]{1,0:T(8,128)S(1)} %columns.3.adjoint, ...), custom_call_target="tpu_custom_call" | custom-call | tf_op jit(solution)/shard_map/forward/pallas_call | solution.py:29
  75.6 5.5 %collective-permute-done.13.refs_1_ = bf16[1024,128]{1,0:T(8,128)(2,1)S(1)} collective-permute-done((bf16[1024,128]{1,0:T(8,128)(2,1)S(1)}, bf16[1024,128]{1,0:T(8,128)(2,1)S(1)}, u32[]{:S(2)}, u32[]{:S(2)}) %collective-permute-start.13) | collective-permute-done | bytes 262176 | tf_op jit(solution)/shard_map/ppermute | solution.py:256
  81.2 3.2 %forward.9 = (f32[2048,128]{1,0:T(8,128)S(1)}, bf16[2048,128]{1,0:T(8,128)(2,1)S(1)}, f32[1024,128]{1,0:T(8,128)S(1)}, bf16[1024,128]{1,0:T(8,128)(2,1)S(1)}) custom-call(s32[2]{0:T(128)S(1)} %pad_add_fusion.refs_0_.index, bf16[2048,2048]{1,0:T(8,128)(2,1)S(1)} %hold.1.z, f32[2048,128]{1,0:T(8,128)S(1)} %columns.2.adjoint, ...), custom_call_target="tpu_custom_call" | custom-call | tf_op jit(solution)/shard_map/forward/pallas_call | solution.py:29
  85.1 2.4 %collective-permute-start.18 = (bf16[1024,128]{1,0:T(8,128)(2,1)S(1)}, bf16[1024,128]{1,0:T(8,128)(2,1)S(1)}, u32[]{:S(2)}, u32[]{:S(2)}) collective-permute-start(bf16[1024,128]{1,0:T(8,128)(2,1)S(1)} %get-tuple-element.250), channel_id=1, source_target_pairs={{0,4},{1,3},{2,6},{3,1},{4,0},{5,7},{6,2},{7,5},{8,12},{9,11},{10,... | collective-permute-start | bytes 786440 | tf_op jit(solution)/shard_map/ppermute | solution.py:286
  90.8 2.4 %collective-permute-done.18.two = bf16[1024,128]{1,0:T(8,128)(2,1)S(1)} collective-permute-done((bf16[1024,128]{1,0:T(8,128)(2,1)S(1)}, bf16[1024,128]{1,0:T(8,128)(2,1)S(1)}, u32[]{:S(2)}, u32[]{:S(2)}) %collective-permute-start.18) | collective-permute-done | bytes 262176 | tf_op jit(solution)/shard_map/ppermute | solution.py:286
  95.2 1.8 collective-permute-start.19
  97.0 2.1 backward.8
  99.4 2.2 %collective-permute-done.19.two = bf16[1024,128]{1,0:T(8,128)(2,1)S(1)} collective-permute-done((bf16[1024,128]{1,0:T(8,128)(2,1)S(1)}, bf16[1024,128]{1,0:T(8,128)(2,1)S(1)}, u32[]{:S(2)}, u32[]{:S(2)}) %collective-permute-start.19) | collective-permute-done | bytes 262176 | tf_op jit(solution)/shard_map/ppermute | solution.py:286
  102.3 4.4 %collective-permute-done.22.two = bf16[1024,128]{1,0:T(8,128)(2,1)S(1)} collective-permute-done((bf16[1024,128]{1,0:T(8,128)(2,1)S(1)}, bf16[1024,128]{1,0:T(8,128)(2,1)S(1)}, u32[]{:S(2)}, u32[]{:S(2)}) %collective-permute-start.22) | collective-permute-done | bytes 262176 | tf_op jit(solution)/shard_map/ppermute | solution.py:256
  108.9 2.1 backward.9
  111.0 1.8 collective-permute-start.23
  114.3 6.5 %collective-permute-done.24.two = bf16[1024,128]{1,0:T(8,128)(2,1)S(1)} collective-permute-done((bf16[1024,128]{1,0:T(8,128)(2,1)S(1)}, bf16[1024,128]{1,0:T(8,128)(2,1)S(1)}, u32[]{:S(2)}, u32[]{:S(2)}) %collective-permute-start.24) | collective-permute-done | bytes 262176 | tf_op jit(solution)/shard_map/ppermute | solution.py:256
  125.0 9.3 %collective-permute-done.26.refs_1_ = bf16[1024,128]{1,0:T(8,128)(2,1)S(1)} collective-permute-done((bf16[1024,128]{1,0:T(8,128)(2,1)S(1)}, bf16[1024,128]{1,0:T(8,128)(2,1)S(1)}, u32[]{:S(2)}, u32[]{:S(2)}) %collective-permute-start.26) | collective-permute-done | bytes 262176 | tf_op jit(solution)/shard_map/ppermute | solution.py:256
  134.3 3.2 %forward.10 = (f32[2048,128]{1,0:T(8,128)S(1)}, bf16[2048,128]{1,0:T(8,128)(2,1)S(1)}, f32[1024,128]{1,0:T(8,128)S(1)}, bf16[1024,128]{1,0:T(8,128)(2,1)S(1)}) custom-call(s32[2]{0:T(128)S(1)} %pad_add_fusion.refs_0_.index, bf16[2048,2048]{1,0:T(8,128)(2,1)S(1)} %hold.1.z, f32[2048,128]{1,0:T(8,128)S(1)} %get-tuple-element.287.adjoint, ...), custom_call_target="tpu_custom_call" | custom-call | tf_op jit(solution)/shard_map/forward/pallas_call | solution.py:29
  139.8 7.2 %collective-permute-done.27.refs_1_ = bf16[1024,128]{1,0:T(8,128)(2,1)S(1)} collective-permute-done((bf16[1024,128]{1,0:T(8,128)(2,1)S(1)}, bf16[1024,128]{1,0:T(8,128)(2,1)S(1)}, u32[]{:S(2)}, u32[]{:S(2)}) %collective-permute-start.27) | collective-permute-done | bytes 262176 | tf_op jit(solution)/shard_map/ppermute | solution.py:256
  147.0 3.2 %forward.11 = (f32[2048,128]{1,0:T(8,128)S(1)}, bf16[2048,128]{1,0:T(8,128)(2,1)S(1)}, f32[1024,128]{1,0:T(8,128)S(1)}, bf16[1024,128]{1,0:T(8,128)(2,1)S(1)}) custom-call(s32[2]{0:T(128)S(1)} %pad_add_fusion.refs_0_.index, bf16[2048,2048]{1,0:T(8,128)(2,1)S(1)} %hold.1.z, f32[2048,128]{1,0:T(8,128)S(1)} %get-tuple-element.297.adjoint, ...), custom_call_target="tpu_custom_call" | custom-call | tf_op jit(solution)/shard_map/forward/pallas_call | solution.py:29
  150.9 3.6 %collective-permute-start.32 = (bf16[1024,128]{1,0:T(8,128)(2,1)S(1)}, bf16[1024,128]{1,0:T(8,128)(2,1)S(1)}, u32[]{:S(2)}, u32[]{:S(2)}) collective-permute-start(bf16[1024,128]{1,0:T(8,128)(2,1)S(1)} %get-tuple-element.306), channel_id=1, source_target_pairs={{0,4},{1,3},{2,6},{3,1},{4,0},{5,7},{6,2},{7,5},{8,12},{9,11},{10,... | collective-permute-start | bytes 786440 | tf_op jit(solution)/shard_map/ppermute | solution.py:286
  157.0 3.7 %collective-permute-done.32.two = bf16[1024,128]{1,0:T(8,128)(2,1)S(1)} collective-permute-done((bf16[1024,128]{1,0:T(8,128)(2,1)S(1)}, bf16[1024,128]{1,0:T(8,128)(2,1)S(1)}, u32[]{:S(2)}, u32[]{:S(2)}) %collective-permute-start.32) | collective-permute-done | bytes 262176 | tf_op jit(solution)/shard_map/ppermute | solution.py:286
  162.2 2.3 %collective-permute-start.33 = (bf16[1024,128]{1,0:T(8,128)(2,1)S(1)}, bf16[1024,128]{1,0:T(8,128)(2,1)S(1)}, u32[]{:S(2)}, u32[]{:S(2)}) collective-permute-start(bf16[1024,128]{1,0:T(8,128)(2,1)S(1)} %get-tuple-element.318), channel_id=1, source_target_pairs={{0,4},{1,3},{2,6},{3,1},{4,0},{5,7},{6,2},{7,5},{8,12},{9,11},{10,... | collective-permute-start | bytes 786440 | tf_op jit(solution)/shard_map/ppermute | solution.py:286
  164.4 2.1 backward.10
  166.9 1.9 collective-permute-done.33.two
  169.5 3.9 %collective-permute-done.36.two = bf16[1024,128]{1,0:T(8,128)(2,1)S(1)} collective-permute-done((bf16[1024,128]{1,0:T(8,128)(2,1)S(1)}, bf16[1024,128]{1,0:T(8,128)(2,1)S(1)}, u32[]{:S(2)}, u32[]{:S(2)}) %collective-permute-start.36) | collective-permute-done | bytes 262176 | tf_op jit(solution)/shard_map/ppermute | solution.py:256
  174.8 2.1 backward.11
  176.9 1.8 collective-permute-start.37
  180.1 5.0 %outer.4.refs_10_ = f32[2048,2048]{1,0:T(8,128)} custom-call(bf16[2048,256]{1,0:T(8,128)(2,1)S(1)} %get-tuple-element.332.refs_0_, bf16[2048,256]{1,0:T(8,128)(2,1)S(1)} %get-tuple-element.333.refs_1_, bf16[2048,256]{1,0:T(8,128)(2,1)S(1)} %get-tuple-element.334.refs_2_, bf16[2048,256]{1,0:T(8,128)(2,1)S(1)} %join.7.refs_3_, ...), custom_call_target="tpu_custom_call" | custom-call | tf_op jit(solution)/shard_map/outer/pallas_call | solution.py:240
  186.9 5.0 %outer.5.refs_10_ = f32[2048,2048]{1,0:T(8,128)} custom-call(bf16[2048,256]{1,0:T(8,128)(2,1)S(1)} %get-tuple-element.332.refs_0_, bf16[2048,256]{1,0:T(8,128)(2,1)S(1)} %get-tuple-element.333.refs_1_, bf16[2048,256]{1,0:T(8,128)(2,1)S(1)} %get-tuple-element.334.refs_2_, bf16[2048,256]{1,0:T(8,128)(2,1)S(1)} %join.7.refs_3_, ...), custom_call_target="tpu_custom_call", output_to_operand_aliasing={{}: (10, {})} | custom-call | tf_op jit(solution)/shard_map/outer/pallas_call | solution.py:240
  192.6 2.4 %collective-permute-start.41 = (bf16[1024,128]{1,0:T(8,128)(2,1)S(1)}, bf16[1024,128]{1,0:T(8,128)(2,1)S(1)}, u32[]{:S(2)}, u32[]{:S(2)}) collective-permute-start(bf16[1024,128]{1,0:T(8,128)(2,1)S(1)} %merge.21.own), channel_id=1, source_target_pairs={{0,8},{8,0},{16,24},{24,16},{1,9},{9,1},{17,25},{25,17},{2,10},{10... | collective-permute-start | bytes 786440 | tf_op jit(solution)/shard_map/ppermute | solution.py:256
  195.0 5.0 %outer.6.refs_10_ = f32[2048,2048]{1,0:T(8,128)} custom-call(bf16[2048,256]{1,0:T(8,128)(2,1)S(1)} %get-tuple-element.332.refs_0_, bf16[2048,256]{1,0:T(8,128)(2,1)S(1)} %get-tuple-element.333.refs_1_, bf16[2048,256]{1,0:T(8,128)(2,1)S(1)} %get-tuple-element.334.refs_2_, bf16[2048,256]{1,0:T(8,128)(2,1)S(1)} %join.7.refs_3_, ...), custom_call_target="tpu_custom_call", output_to_operand_aliasing={{}: (10, {})} | custom-call | tf_op jit(solution)/shard_map/outer/pallas_call | solution.py:240
  200.0 6.2 %collective-permute-done.39.two = bf16[1024,128]{1,0:T(8,128)(2,1)S(1)} collective-permute-done((bf16[1024,128]{1,0:T(8,128)(2,1)S(1)}, bf16[1024,128]{1,0:T(8,128)(2,1)S(1)}, u32[]{:S(2)}, u32[]{:S(2)}) %collective-permute-start.39) | collective-permute-done | bytes 262176 | tf_op jit(solution)/shard_map/ppermute | solution.py:256
  206.9 5.0 %outer.7 = f32[2048,2048]{1,0:T(8,128)} custom-call(bf16[2048,256]{1,0:T(8,128)(2,1)S(1)} %get-tuple-element.332.refs_0_, bf16[2048,256]{1,0:T(8,128)(2,1)S(1)} %get-tuple-element.333.refs_1_, bf16[2048,256]{1,0:T(8,128)(2,1)S(1)} %get-tuple-element.334.refs_2_, bf16[2048,256]{1,0:T(8,128)(2,1)S(1)} %join.7.refs_3_, ...), custom_call_target="tpu_custom_call", output_to_operand_aliasing={{}: (10, {})} | custom-call | tf_op jit(solution)/shard_map/outer/pallas_call | solution.py:240
  211.9 1.6 finish.2.refs_0_
  215.0 1.6 finish.3
  (110 shorter events, 51.3 us)
Async XLA Ops:
  0.6 1.6 copy-start.2
  5.8 8.4 %copy-start.3 = (f32[2048,256]{1,0:T(8,128)S(1)}, f32[2048,256]{1,0:T(8,128)}, u32[]{:S(2)}) copy-start(f32[2048,256]{1,0:T(8,128)} %start.3) | copy-start | bytes 6291460
  8.9 14.5 %slice-start = ((s8[6291456]{0:T(1024)(128)(4,1)}), s8[4194304]{0:T(1024)(128)(4,1)S(1)}, s32[]{:S(2)}) async-start(s8[6291456]{0:T(1024)(128)(4,1)} %bitcast.2), calls=%async_computation | async-start | bytes 8388608
  8.9 14.5 %copy-start.1 = (s32[2048,256]{1,0:T(8,128)S(1)}, s32[2048,256]{1,0:T(8,128)}, u32[]{:S(2)}) copy-start(s32[2048,256]{1,0:T(8,128)} %labels.5) | copy-start | bytes 6291460
  8.9 1.7 collective-permute-start
  11.2 7.3 %collective-permute-start.2 = (bf16[1024,128]{1,0:T(8,128)(2,1)S(1)}, bf16[1024,128]{1,0:T(8,128)(2,1)S(1)}, u32[]{:S(2)}, u32[]{:S(2)}) collective-permute-start(bf16[1024,128]{1,0:T(8,128)(2,1)S(1)} %get-tuple-element.188), channel_id=1, source_target_pairs={{0,2},{1,5},{2,0},{3,7},{4,6},{5,1},{6,4},{7,3},{8,10},{9,13},{10,... | collective-permute-start | bytes 786440 | tf_op jit(solution)/shard_map/ppermute | solution.py:286
  14.2 9.2 %slice-start.1 = ((s8[6291456]{0:T(1024)(128)(4,1)}), s8[2097152]{0:T(1024)(128)(4,1)S(1)}, s32[]{:S(2)}) async-start(s8[6291456]{0:T(1024)(128)(4,1)} %bitcast.2), calls=%async_computation.1 | async-start | bytes 4194304
  17.3 3.9 %collective-permute-start.1 = (bf16[1024,128]{1,0:T(8,128)(2,1)S(1)}, bf16[1024,128]{1,0:T(8,128)(2,1)S(1)}, u32[]{:S(2)}, u32[]{:S(2)}) collective-permute-start(bf16[1024,128]{1,0:T(8,128)(2,1)S(1)} %get-tuple-element.191), channel_id=1, source_target_pairs={{0,1},{1,0},{2,3},{3,2},{4,5},{5,4},{6,7},{7,6},{8,9},{9,8},{10,11... | collective-permute-start | bytes 786440 | tf_op jit(solution)/shard_map/ppermute | solution.py:256
  19.1 8.6 %collective-permute-start.4 = (bf16[1024,128]{1,0:T(8,128)(2,1)S(1)}, bf16[1024,128]{1,0:T(8,128)(2,1)S(1)}, u32[]{:S(2)}, u32[]{:S(2)}) collective-permute-start(bf16[1024,128]{1,0:T(8,128)(2,1)S(1)} %get-tuple-element.195), channel_id=1, source_target_pairs={{0,4},{1,3},{2,6},{3,1},{4,0},{5,7},{6,2},{7,5},{8,12},{9,11},{10,... | collective-permute-start | bytes 786440 | tf_op jit(solution)/shard_map/ppermute | solution.py:286
  21.9 6.6 %collective-permute-start.3 = (bf16[1024,128]{1,0:T(8,128)(2,1)S(1)}, bf16[1024,128]{1,0:T(8,128)(2,1)S(1)}, u32[]{:S(2)}, u32[]{:S(2)}) collective-permute-start(bf16[1024,128]{1,0:T(8,128)(2,1)S(1)} %get-tuple-element.199), channel_id=1, source_target_pairs={{0,2},{1,5},{2,0},{3,7},{4,6},{5,1},{6,4},{7,3},{8,10},{9,13},{10,... | collective-permute-start | bytes 786440 | tf_op jit(solution)/shard_map/ppermute | solution.py:286
  28.4 3.3 %collective-permute-start.6 = (bf16[1024,128]{1,0:T(8,128)(2,1)S(1)}, bf16[1024,128]{1,0:T(8,128)(2,1)S(1)}, u32[]{:S(2)}, u32[]{:S(2)}) collective-permute-start(bf16[1024,128]{1,0:T(8,128)(2,1)S(1)} %weigh.6.w_own), channel_id=1, source_target_pairs={{0,1},{1,0},{2,3},{3,2},{4,5},{5,4},{6,7},{7,6},{8,9},{9,8},{10,11... | collective-permute-start | bytes 786440 | tf_op jit(solution)/shard_map/ppermute | solution.py:256
  29.1 6.9 %collective-permute-start.5 = (bf16[1024,128]{1,0:T(8,128)(2,1)S(1)}, bf16[1024,128]{1,0:T(8,128)(2,1)S(1)}, u32[]{:S(2)}, u32[]{:S(2)}) collective-permute-start(bf16[1024,128]{1,0:T(8,128)(2,1)S(1)} %get-tuple-element.207), channel_id=1, source_target_pairs={{0,4},{1,3},{2,6},{3,1},{4,0},{5,7},{6,2},{7,5},{8,12},{9,11},{10,... | collective-permute-start | bytes 786440 | tf_op jit(solution)/shard_map/ppermute | solution.py:286
  33.7 7.8 %collective-permute-start.8 = (bf16[1024,128]{1,0:T(8,128)(2,1)S(1)}, bf16[1024,128]{1,0:T(8,128)(2,1)S(1)}, u32[]{:S(2)}, u32[]{:S(2)}) collective-permute-start(bf16[1024,128]{1,0:T(8,128)(2,1)S(1)} %get-tuple-element.214), channel_id=1, source_target_pairs={{0,8},{8,0},{16,24},{24,16},{1,9},{9,1},{17,25},{25,17},{2,10},{10... | collective-permute-start | bytes 786440 | tf_op jit(solution)/shard_map/ppermute | solution.py:256
  36.6 8.3 %collective-permute-start.7 = (bf16[1024,128]{1,0:T(8,128)(2,1)S(1)}, bf16[1024,128]{1,0:T(8,128)(2,1)S(1)}, u32[]{:S(2)}, u32[]{:S(2)}) collective-permute-start(bf16[1024,128]{1,0:T(8,128)(2,1)S(1)} %weigh.7.w_own), channel_id=1, source_target_pairs={{0,1},{1,0},{2,3},{3,2},{4,5},{5,4},{6,7},{7,6},{8,9},{9,8},{10,11... | collective-permute-start | bytes 786440 | tf_op jit(solution)/shard_map/ppermute | solution.py:256
  42.1 13.8 %collective-permute-start.10 = (bf16[1024,128]{1,0:T(8,128)(2,1)S(1)}, bf16[1024,128]{1,0:T(8,128)(2,1)S(1)}, u32[]{:S(2)}, u32[]{:S(2)}) collective-permute-start(bf16[1024,128]{1,0:T(8,128)(2,1)S(1)} %merge.12.one), channel_id=1, source_target_pairs={{0,16},{8,24},{16,0},{24,8},{1,17},{9,25},{17,1},{25,9},{2,18},{10... | collective-permute-start | bytes 786440 | tf_op jit(solution)/shard_map/ppermute | solution.py:256
  47.0 11.2 %collective-permute-start.9 = (bf16[1024,128]{1,0:T(8,128)(2,1)S(1)}, bf16[1024,128]{1,0:T(8,128)(2,1)S(1)}, u32[]{:S(2)}, u32[]{:S(2)}) collective-permute-start(bf16[1024,128]{1,0:T(8,128)(2,1)S(1)} %get-tuple-element.220), channel_id=1, source_target_pairs={{0,8},{8,0},{16,24},{24,16},{1,9},{9,1},{17,25},{25,17},{2,10},{10... | collective-permute-start | bytes 786440 | tf_op jit(solution)/shard_map/ppermute | solution.py:256
  56.4 12.0 %collective-permute-start.12 = (bf16[1024,128]{1,0:T(8,128)(2,1)S(1)}, bf16[1024,128]{1,0:T(8,128)(2,1)S(1)}, u32[]{:S(2)}, u32[]{:S(2)}) collective-permute-start(bf16[1024,128]{1,0:T(8,128)(2,1)S(1)} %merge.13.refs_0_), channel_id=1, source_target_pairs={{0,8},{8,0},{16,24},{24,16},{1,9},{9,1},{17,25},{25,17},{2,10},{10... | collective-permute-start | bytes 786440 | tf_op jit(solution)/shard_map/ppermute | solution.py:256
  58.8 14.3 %collective-permute-start.11 = (bf16[1024,128]{1,0:T(8,128)(2,1)S(1)}, bf16[1024,128]{1,0:T(8,128)(2,1)S(1)}, u32[]{:S(2)}, u32[]{:S(2)}) collective-permute-start(bf16[1024,128]{1,0:T(8,128)(2,1)S(1)} %merge.14.one), channel_id=1, source_target_pairs={{0,16},{8,24},{16,0},{24,8},{1,17},{9,25},{17,1},{25,9},{2,18},{10... | collective-permute-start | bytes 786440 | tf_op jit(solution)/shard_map/ppermute | solution.py:256
  71.7 2.1 collective-permute-start.14
  73.7 7.5 %collective-permute-start.13 = (bf16[1024,128]{1,0:T(8,128)(2,1)S(1)}, bf16[1024,128]{1,0:T(8,128)(2,1)S(1)}, u32[]{:S(2)}, u32[]{:S(2)}) collective-permute-start(bf16[1024,128]{1,0:T(8,128)(2,1)S(1)} %merge.15.refs_0_), channel_id=1, source_target_pairs={{0,8},{8,0},{16,24},{24,16},{1,9},{9,1},{17,25},{25,17},{2,10},{10... | collective-permute-start | bytes 786440 | tf_op jit(solution)/shard_map/ppermute | solution.py:256
  74.4 10.0 %collective-permute-start.16 = (bf16[1024,128]{1,0:T(8,128)(2,1)S(1)}, bf16[1024,128]{1,0:T(8,128)(2,1)S(1)}, u32[]{:S(2)}, u32[]{:S(2)}) collective-permute-start(bf16[1024,128]{1,0:T(8,128)(2,1)S(1)} %get-tuple-element.240), channel_id=1, source_target_pairs={{0,2},{1,5},{2,0},{3,7},{4,6},{5,1},{6,4},{7,3},{8,10},{9,13},{10,... | collective-permute-start | bytes 786440 | tf_op jit(solution)/shard_map/ppermute | solution.py:286
  84.4 3.1 %collective-permute-start.15 = (bf16[1024,128]{1,0:T(8,128)(2,1)S(1)}, bf16[1024,128]{1,0:T(8,128)(2,1)S(1)}, u32[]{:S(2)}, u32[]{:S(2)}) collective-permute-start(bf16[1024,128]{1,0:T(8,128)(2,1)S(1)} %get-tuple-element.246), channel_id=1, source_target_pairs={{0,1},{1,0},{2,3},{3,2},{4,5},{5,4},{6,7},{7,6},{8,9},{9,8},{10,11... | collective-permute-start | bytes 786440 | tf_op jit(solution)/shard_map/ppermute | solution.py:256
  85.1 8.1 %collective-permute-start.18 = (bf16[1024,128]{1,0:T(8,128)(2,1)S(1)}, bf16[1024,128]{1,0:T(8,128)(2,1)S(1)}, u32[]{:S(2)}, u32[]{:S(2)}) collective-permute-start(bf16[1024,128]{1,0:T(8,128)(2,1)S(1)} %get-tuple-element.250), channel_id=1, source_target_pairs={{0,4},{1,3},{2,6},{3,1},{4,0},{5,7},{6,2},{7,5},{8,12},{9,11},{10,... | collective-permute-start | bytes 786440 | tf_op jit(solution)/shard_map/ppermute | solution.py:286
  88.1 6.4 %collective-permute-start.17 = (bf16[1024,128]{1,0:T(8,128)(2,1)S(1)}, bf16[1024,128]{1,0:T(8,128)(2,1)S(1)}, u32[]{:S(2)}, u32[]{:S(2)}) collective-permute-start(bf16[1024,128]{1,0:T(8,128)(2,1)S(1)} %get-tuple-element.254), channel_id=1, source_target_pairs={{0,2},{1,5},{2,0},{3,7},{4,6},{5,1},{6,4},{7,3},{8,10},{9,13},{10,... | collective-permute-start | bytes 786440 | tf_op jit(solution)/shard_map/ppermute | solution.py:286
  93.8 3.1 %collective-permute-start.20 = (bf16[1024,128]{1,0:T(8,128)(2,1)S(1)}, bf16[1024,128]{1,0:T(8,128)(2,1)S(1)}, u32[]{:S(2)}, u32[]{:S(2)}) collective-permute-start(bf16[1024,128]{1,0:T(8,128)(2,1)S(1)} %weigh.8.w_own), channel_id=1, source_target_pairs={{0,1},{1,0},{2,3},{3,2},{4,5},{5,4},{6,7},{7,6},{8,9},{9,8},{10,11... | collective-permute-start | bytes 786440 | tf_op jit(solution)/shard_map/ppermute | solution.py:256
  95.2 6.4 %collective-permute-start.19 = (bf16[1024,128]{1,0:T(8,128)(2,1)S(1)}, bf16[1024,128]{1,0:T(8,128)(2,1)S(1)}, u32[]{:S(2)}, u32[]{:S(2)}) collective-permute-start(bf16[1024,128]{1,0:T(8,128)(2,1)S(1)} %get-tuple-element.262), channel_id=1, source_target_pairs={{0,4},{1,3},{2,6},{3,1},{4,0},{5,7},{6,2},{7,5},{8,12},{9,11},{10,... | collective-permute-start | bytes 786440 | tf_op jit(solution)/shard_map/ppermute | solution.py:286
  99.0 7.7 %collective-permute-start.22 = (bf16[1024,128]{1,0:T(8,128)(2,1)S(1)}, bf16[1024,128]{1,0:T(8,128)(2,1)S(1)}, u32[]{:S(2)}, u32[]{:S(2)}) collective-permute-start(bf16[1024,128]{1,0:T(8,128)(2,1)S(1)} %get-tuple-element.269), channel_id=1, source_target_pairs={{0,8},{8,0},{16,24},{24,16},{1,9},{9,1},{17,25},{25,17},{2,10},{10... | collective-permute-start | bytes 786440 | tf_op jit(solution)/shard_map/ppermute | solution.py:256
  102.3 6.7 %collective-permute-start.21 = (bf16[1024,128]{1,0:T(8,128)(2,1)S(1)}, bf16[1024,128]{1,0:T(8,128)(2,1)S(1)}, u32[]{:S(2)}, u32[]{:S(2)}) collective-permute-start(bf16[1024,128]{1,0:T(8,128)(2,1)S(1)} %weigh.9.w_own), channel_id=1, source_target_pairs={{0,1},{1,0},{2,3},{3,2},{4,5},{5,4},{6,7},{7,6},{8,9},{9,8},{10,11... | collective-permute-start | bytes 786440 | tf_op jit(solution)/shard_map/ppermute | solution.py:256
  107.3 13.4 %collective-permute-start.24 = (bf16[1024,128]{1,0:T(8,128)(2,1)S(1)}, bf16[1024,128]{1,0:T(8,128)(2,1)S(1)}, u32[]{:S(2)}, u32[]{:S(2)}) collective-permute-start(bf16[1024,128]{1,0:T(8,128)(2,1)S(1)} %merge.16.one), channel_id=1, source_target_pairs={{0,16},{8,24},{16,0},{24,8},{1,17},{9,25},{17,1},{25,9},{2,18},{10... | collective-permute-start | bytes 786440 | tf_op jit(solution)/shard_map/ppermute | solution.py:256
  111.0 11.9 %collective-permute-start.23 = (bf16[1024,128]{1,0:T(8,128)(2,1)S(1)}, bf16[1024,128]{1,0:T(8,128)(2,1)S(1)}, u32[]{:S(2)}, u32[]{:S(2)}) collective-permute-start(bf16[1024,128]{1,0:T(8,128)(2,1)S(1)} %get-tuple-element.275), channel_id=1, source_target_pairs={{0,8},{8,0},{16,24},{24,16},{1,9},{9,1},{17,25},{25,17},{2,10},{10... | collective-permute-start | bytes 786440 | tf_op jit(solution)/shard_map/ppermute | solution.py:256
  121.3 12.9 %collective-permute-start.26 = (bf16[1024,128]{1,0:T(8,128)(2,1)S(1)}, bf16[1024,128]{1,0:T(8,128)(2,1)S(1)}, u32[]{:S(2)}, u32[]{:S(2)}) collective-permute-start(bf16[1024,128]{1,0:T(8,128)(2,1)S(1)} %merge.17.refs_0_), channel_id=1, source_target_pairs={{0,8},{8,0},{16,24},{24,16},{1,9},{9,1},{17,25},{25,17},{2,10},{10... | collective-permute-start | bytes 786440 | tf_op jit(solution)/shard_map/ppermute | solution.py:256
  123.5 14.0 %collective-permute-start.25 = (bf16[1024,128]{1,0:T(8,128)(2,1)S(1)}, bf16[1024,128]{1,0:T(8,128)(2,1)S(1)}, u32[]{:S(2)}, u32[]{:S(2)}) collective-permute-start(bf16[1024,128]{1,0:T(8,128)(2,1)S(1)} %merge.18.one), channel_id=1, source_target_pairs={{0,16},{8,24},{16,0},{24,8},{1,17},{9,25},{17,1},{25,9},{2,18},{10... | collective-permute-start | bytes 786440 | tf_op jit(solution)/shard_map/ppermute | solution.py:256
  137.5 1.6 collective-permute-start.28
  138.2 8.8 %collective-permute-start.27 = (bf16[1024,128]{1,0:T(8,128)(2,1)S(1)}, bf16[1024,128]{1,0:T(8,128)(2,1)S(1)}, u32[]{:S(2)}, u32[]{:S(2)}) collective-permute-start(bf16[1024,128]{1,0:T(8,128)(2,1)S(1)} %merge.19.refs_0_), channel_id=1, source_target_pairs={{0,8},{8,0},{16,24},{24,16},{1,9},{9,1},{17,25},{25,17},{2,10},{10... | collective-permute-start | bytes 786440 | tf_op jit(solution)/shard_map/ppermute | solution.py:256
  139.7 10.5 %collective-permute-start.30 = (bf16[1024,128]{1,0:T(8,128)(2,1)S(1)}, bf16[1024,128]{1,0:T(8,128)(2,1)S(1)}, u32[]{:S(2)}, u32[]{:S(2)}) collective-permute-start(bf16[1024,128]{1,0:T(8,128)(2,1)S(1)} %get-tuple-element.296), channel_id=1, source_target_pairs={{0,2},{1,5},{2,0},{3,7},{4,6},{5,1},{6,4},{7,3},{8,10},{9,13},{10,... | collective-permute-start | bytes 786440 | tf_op jit(solution)/shard_map/ppermute | solution.py:286
  150.2 4.3 %collective-permute-start.29 = (bf16[1024,128]{1,0:T(8,128)(2,1)S(1)}, bf16[1024,128]{1,0:T(8,128)(2,1)S(1)}, u32[]{:S(2)}, u32[]{:S(2)}) collective-permute-start(bf16[1024,128]{1,0:T(8,128)(2,1)S(1)} %get-tuple-element.302), channel_id=1, source_target_pairs={{0,1},{1,0},{2,3},{3,2},{4,5},{5,4},{6,7},{7,6},{8,9},{9,8},{10,11... | collective-permute-start | bytes 786440 | tf_op jit(solution)/shard_map/ppermute | solution.py:256
  150.9 9.8 %collective-permute-start.32 = (bf16[1024,128]{1,0:T(8,128)(2,1)S(1)}, bf16[1024,128]{1,0:T(8,128)(2,1)S(1)}, u32[]{:S(2)}, u32[]{:S(2)}) collective-permute-start(bf16[1024,128]{1,0:T(8,128)(2,1)S(1)} %get-tuple-element.306), channel_id=1, source_target_pairs={{0,4},{1,3},{2,6},{3,1},{4,0},{5,7},{6,2},{7,5},{8,12},{9,11},{10,... | collective-permute-start | bytes 786440 | tf_op jit(solution)/shard_map/ppermute | solution.py:286
  155.1 6.4 %collective-permute-start.31 = (bf16[1024,128]{1,0:T(8,128)(2,1)S(1)}, bf16[1024,128]{1,0:T(8,128)(2,1)S(1)}, u32[]{:S(2)}, u32[]{:S(2)}) collective-permute-start(bf16[1024,128]{1,0:T(8,128)(2,1)S(1)} %get-tuple-element.310), channel_id=1, source_target_pairs={{0,2},{1,5},{2,0},{3,7},{4,6},{5,1},{6,4},{7,3},{8,10},{9,13},{10,... | collective-permute-start | bytes 786440 | tf_op jit(solution)/shard_map/ppermute | solution.py:286
  161.3 3.1 %collective-permute-start.34 = (bf16[1024,128]{1,0:T(8,128)(2,1)S(1)}, bf16[1024,128]{1,0:T(8,128)(2,1)S(1)}, u32[]{:S(2)}, u32[]{:S(2)}) collective-permute-start(bf16[1024,128]{1,0:T(8,128)(2,1)S(1)} %weigh.10.w_own), channel_id=1, source_target_pairs={{0,1},{1,0},{2,3},{3,2},{4,5},{5,4},{6,7},{7,6},{8,9},{9,8},{10,11... | collective-permute-start | bytes 786440 | tf_op jit(solution)/shard_map/ppermute | solution.py:256
  162.2 6.6 %collective-permute-start.33 = (bf16[1024,128]{1,0:T(8,128)(2,1)S(1)}, bf16[1024,128]{1,0:T(8,128)(2,1)S(1)}, u32[]{:S(2)}, u32[]{:S(2)}) collective-permute-start(bf16[1024,128]{1,0:T(8,128)(2,1)S(1)} %get-tuple-element.318), channel_id=1, source_target_pairs={{0,4},{1,3},{2,6},{3,1},{4,0},{5,7},{6,2},{7,5},{8,12},{9,11},{10,... | collective-permute-start | bytes 786440 | tf_op jit(solution)/shard_map/ppermute | solution.py:286
  166.5 13.6 %copy-start = (bf16[3,2048,256]{2,1,0:T(8,128)(2,1)S(1)}, bf16[3,2048,256]{2,1,0:T(8,128)(2,1)}, u32[]{:S(2)}) copy-start(bf16[3,2048,256]{2,1,0:T(8,128)(2,1)} %refs_9_.7) | copy-start | bytes 9437188
  166.5 6.9 %collective-permute-start.36 = (bf16[1024,128]{1,0:T(8,128)(2,1)S(1)}, bf16[1024,128]{1,0:T(8,128)(2,1)S(1)}, u32[]{:S(2)}, u32[]{:S(2)}) collective-permute-start(bf16[1024,128]{1,0:T(8,128)(2,1)S(1)} %get-tuple-element.325), channel_id=1, source_target_pairs={{0,8},{8,0},{16,24},{24,16},{1,9},{9,1},{17,25},{25,17},{2,10},{10... | collective-permute-start | bytes 786440 | tf_op jit(solution)/shard_map/ppermute | solution.py:256
  169.4 5.4 %collective-permute-start.35 = (bf16[1024,128]{1,0:T(8,128)(2,1)S(1)}, bf16[1024,128]{1,0:T(8,128)(2,1)S(1)}, u32[]{:S(2)}, u32[]{:S(2)}) collective-permute-start(bf16[1024,128]{1,0:T(8,128)(2,1)S(1)} %weigh.11.w_own), channel_id=1, source_target_pairs={{0,1},{1,0},{2,3},{3,2},{4,5},{5,4},{6,7},{7,6},{8,9},{9,8},{10,11... | collective-permute-start | bytes 786440 | tf_op jit(solution)/shard_map/ppermute | solution.py:256
  174.0 12.3 %collective-permute-start.38 = (bf16[1024,128]{1,0:T(8,128)(2,1)S(1)}, bf16[1024,128]{1,0:T(8,128)(2,1)S(1)}, u32[]{:S(2)}, u32[]{:S(2)}) collective-permute-start(bf16[1024,128]{1,0:T(8,128)(2,1)S(1)} %merge.20.one), channel_id=1, source_target_pairs={{0,16},{8,24},{16,0},{24,8},{1,17},{9,25},{17,1},{25,9},{2,18},{10... | collective-permute-start | bytes 786440 | tf_op jit(solution)/shard_map/ppermute | solution.py:256
  176.9 15.1 %collective-permute-start.37 = (bf16[1024,128]{1,0:T(8,128)(2,1)S(1)}, bf16[1024,128]{1,0:T(8,128)(2,1)S(1)}, u32[]{:S(2)}, u32[]{:S(2)}) collective-permute-start(bf16[1024,128]{1,0:T(8,128)(2,1)S(1)} %get-tuple-element.331), channel_id=1, source_target_pairs={{0,8},{8,0},{16,24},{24,16},{1,9},{9,1},{17,25},{25,17},{2,10},{10... | collective-permute-start | bytes 786440 | tf_op jit(solution)/shard_map/ppermute | solution.py:256
  192.5 13.6 %collective-permute-start.39 = (bf16[1024,128]{1,0:T(8,128)(2,1)S(1)}, bf16[1024,128]{1,0:T(8,128)(2,1)S(1)}, u32[]{:S(2)}, u32[]{:S(2)}) collective-permute-start(bf16[1024,128]{1,0:T(8,128)(2,1)S(1)} %merge.22.one), channel_id=1, source_target_pairs={{0,16},{8,24},{16,0},{24,8},{1,17},{9,25},{17,1},{25,9},{2,18},{10... | collective-permute-start | bytes 786440 | tf_op jit(solution)/shard_map/ppermute | solution.py:256
  192.6 19.2 %collective-permute-start.41 = (bf16[1024,128]{1,0:T(8,128)(2,1)S(1)}, bf16[1024,128]{1,0:T(8,128)(2,1)S(1)}, u32[]{:S(2)}, u32[]{:S(2)}) collective-permute-start(bf16[1024,128]{1,0:T(8,128)(2,1)S(1)} %merge.21.own), channel_id=1, source_target_pairs={{0,8},{8,0},{16,24},{24,16},{1,9},{9,1},{17,25},{25,17},{2,10},{10... | collective-permute-start | bytes 786440 | tf_op jit(solution)/shard_map/ppermute | solution.py:256
  206.8 8.2 %collective-permute-start.40 = (bf16[1024,128]{1,0:T(8,128)(2,1)S(1)}, bf16[1024,128]{1,0:T(8,128)(2,1)S(1)}, u32[]{:S(2)}, u32[]{:S(2)}) collective-permute-start(bf16[1024,128]{1,0:T(8,128)(2,1)S(1)} %merge.23.own), channel_id=1, source_target_pairs={{0,8},{8,0},{16,24},{24,16},{1,9},{9,1},{17,25},{25,17},{2,10},{10... | collective-permute-start | bytes 786440 | tf_op jit(solution)/shard_map/ppermute | solution.py:256
